TPU v7x, 256 devices: a whole 4x4x8 slice. The times are simulated.
256 devices in a mesh: row: 16 (over x, y), col: 16 (over z, core).
Axes of the slice: x: 4, y: 4, z: 8, core: 2. Of those that a mesh axis runs over, the one named last changes fastest.
Arguments:
- tokens: bfloat16 [512, 16384], P('col', 'row'), may hold values from -6 to 6
- cotangent: bfloat16 [512, 16384], P('col', 'row'), may hold values from -6 to 6
- gate_weight: bfloat16 [16384, 26624], P('row', 'col'), may hold values from -0.046875 to 0.046875
- up_weight: bfloat16 [16384, 26624], P('row', 'col'), may hold values from -0.046875 to 0.046875
- down_weight: bfloat16 [26624, 16384], P('col', 'row'), may hold values from -0.0390625 to 0.0390625
Outputs:
- output: bfloat16 [512, 16384], P('col', 'row')
- input_grad: bfloat16 [512, 16384], P('col', 'row')
All inputs are finite; a program needn't handle non-finite values.
Results may differ from a plain program's by a relative error of at most 0.005.
Values may be sent and summed in bfloat16 or wider, within the bound.
A program may use at most 128 MiB of HBM per device.

v0:
```python
import jax
import jax.numpy as jnp
from jax import lax
from jax.sharding import PartitionSpec as P


def transposed(left, right):
    return lax.dot_general(
        left, right, (((1,), (1,)), ((), ())), preferred_element_type=jnp.float32
    )


def body(tokens, cotangent, gate_weight, up_weight, down_weight):
    hidden_width = gate_weight.shape[1]
    seen_tokens = lax.all_gather(tokens, "col", axis=0, tiled=True)
    block = seen_tokens
    gate_part = jnp.dot(block, gate_weight, preferred_element_type=jnp.float32)
    up_part = jnp.dot(block, up_weight, preferred_element_type=jnp.float32)
    summed = lax.psum_scatter(
        jnp.concatenate((gate_part, up_part), axis=1), "row", scatter_dimension=0, tiled=True
    )
    gate = summed[:, :hidden_width]
    up = summed[:, hidden_width:]
    sigmoid_gate = jax.nn.sigmoid(gate)
    hidden = (gate * sigmoid_gate * up).astype(jnp.bfloat16)
    output_terms = jnp.dot(
        lax.all_gather(hidden, "row", axis=0, tiled=True),
        down_weight,
        preferred_element_type=jnp.float32,
    )
    output = lax.psum_scatter(output_terms, "col", scatter_dimension=0, tiled=True).astype(
        jnp.bfloat16
    )
    seen_grads = lax.all_gather(cotangent, "col", axis=0, tiled=True)
    block = seen_grads
    hidden_grad = lax.psum_scatter(
        transposed(block, down_weight), "row", scatter_dimension=0, tiled=True
    )
    gate_grad = (hidden_grad * up * sigmoid_gate * (1.0 + gate * (1.0 - sigmoid_gate))).astype(
        jnp.bfloat16
    )
    up_grad = (hidden_grad * gate * sigmoid_gate).astype(jnp.bfloat16)
    stacked_grads = jnp.concatenate((gate_grad, up_grad), axis=1)
    piece_rows = lax.all_gather(stacked_grads, "row", axis=0, tiled=True)
    grad_terms = transposed(piece_rows[:, :hidden_width], gate_weight) + transposed(
        piece_rows[:, hidden_width:], up_weight
    )
    input_grad = lax.psum_scatter(grad_terms, "col", scatter_dimension=0, tiled=True).astype(
        jnp.bfloat16
    )
    return (output, input_grad)


def solution(mesh):
    placed = (P("col", "row"), P("col", "row"), P("row", "col"), P("row", "col"), P("col", "row"))
    return jax.shard_map(
        body,
        mesh=mesh,
        in_specs=placed,
        out_specs=(P("col", "row"), P("col", "row")),
        check_vma=False,
    )
```

profile of v0, /device:TPU:1, one launch (start us, length us, event | category | flops | bytes accessed | tf_op | source)
XLA Modules:
  0.0 499.4 jit_solution(17659887186129679838)
XLA Ops:
  7.2 0.0 copy-start
  7.2 0.0 all-gather.9.cloned.1.call-start
  7.2 0.7 all-gather.9.cloned.1.call-update
  7.9 0.0 all-gather.5.cloned.1.call-start
  8.0 0.7 all-gather.5.cloned.1.call-update
  8.7 0.0 reduce-scatter.9.cloned.1.call-start
  8.7 44.0 %all-gather.9.cloned.1.call-done = bf16[512,1024]{1,0:T(8,128)(2,1)} async-done(((bf16[32,1024]{1,0:T(8,128)(2,1)}), bf16[512,1024]{1,0:T(8,128)(2,1)}) %all-gather.9.cloned.1.call-update) | async-done | bytes 1048592 | tf_op jit(solution)/shard_map/all_gather | solution.py:34
  52.7 0.0 copy-done
  52.7 5.1 %fusion.10 = f32[512,1664]{1,0:T(8,128)} fusion(bf16[512,1024]{1,0:T(8,128)(2,1)} %all-gather.9.cloned.1.call-done, bf16[1664,1024]{1,0:T(8,128)(2,1)S(1)} %copy-done), kind=kOutput, calls=%fused_computation.14 | convolution fusion | flops 1744830464 | bytes 7864320 | tf_op jit(solution)/shard_map/dot_general | solution.py:8
  57.8 0.0 reduce-scatter.9.cloned.1.call-update
  57.8 0.0 reduce-scatter.5.cloned.1.call-start
  57.9 33.9 %all-gather.5.cloned.1.call-done = bf16[512,1024]{1,0:T(8,128)(2,1)} async-done(((bf16[32,1024]{1,0:T(8,128)(2,1)}), bf16[512,1024]{1,0:T(8,128)(2,1)}) %all-gather.5.cloned.1.call-update) | async-done | bytes 1048592 | tf_op jit(solution)/shard_map/all_gather | solution.py:15
  91.8 0.0 copy-start.1
  91.8 0.0 copy-start.4
  91.8 4.5 fusion.7
  96.3 0.0 copy-done.1
  96.3 0.0 copy-done.4
  96.3 2.1 fusion.8
  98.4 3.3 pad_maximum_fusion
  101.7 0.0 reduce-scatter.5.cloned.1.call-update
  101.8 0.0 all-gather.7.cloned.1.call-start
  101.8 71.4 %reduce-scatter.9.cloned.1.call-done = f32[32,1664]{1,0:T(8,128)} async-done(((f32[512,1664]{1,0:T(8,128)}), f32[32,1664]{1,0:T(8,128)}) %reduce-scatter.9.cloned.1.call-update) | async-done | bytes 213008 | tf_op jit(solution)/shard_map/reduce_scatter | solution.py:36
  173.2 90.9 %reduce-scatter.5.cloned.1.call-done = f32[32,3328]{1,0:T(8,128)} async-done(((f32[512,3328]{1,0:T(8,128)}), f32[32,3328]{1,0:T(8,128)}) %reduce-scatter.5.cloned.1.call-update) | async-done | bytes 426000 | tf_op jit(solution)/shard_map/reduce_scatter | solution.py:19
  264.1 1.9 multiply_convert_fusion.1
  266.1 0.0 all-gather.7.cloned.1.call-update
  266.1 0.0 all-gather.11.cloned.1.call-start
  266.1 1.6 pad_maximum_fusion.1
  267.7 0.0 all-gather.11.cloned.1.call-update
  267.8 0.0 reduce-scatter.7.cloned.1.call-start
  267.8 47.6 %all-gather.7.cloned.1.call-done = bf16[512,1664]{1,0:T(8,128)(2,1)} async-done(((bf16[32,1664]{1,0:T(8,128)(2,1)}), bf16[512,1664]{1,0:T(8,128)(2,1)}) %all-gather.7.cloned.1.call-update) | async-done | bytes 1703952 | tf_op jit(solution)/shard_map/all_gather | solution.py:27
  315.4 4.9 fusion.9
  320.3 0.0 reduce-scatter.7.cloned.1.call-update
  320.3 0.0 reduce-scatter.11.cloned.1.call-start
  320.4 51.7 %all-gather.11.cloned.1.call-done = bf16[512,3328]{1,0:T(8,128)(2,1)} async-done(((bf16[32,3328]{1,0:T(8,128)(2,1)}), bf16[512,3328]{1,0:T(8,128)(2,1)}) %all-gather.11.cloned.1.call-update) | async-done | bytes 3407888 | tf_op jit(solution)/shard_map/all_gather | solution.py:44
  372.1 0.0 copy-start.2
  372.1 0.0 copy-start.3
  372.1 4.7 fusion
  376.8 0.0 copy-done.2
  376.8 0.0 copy-done.3
  376.8 3.4 fusion.4
  380.2 0.0 reduce-scatter.11.cloned.1.call-update
  380.3 50.2 %reduce-scatter.7.cloned.1.call-done = f32[32,1024]{1,0:T(8,128)} async-done(((f32[512,1024]{1,0:T(8,128)}), f32[32,1024]{1,0:T(8,128)}) %reduce-scatter.7.cloned.1.call-update) | async-done | bytes 131088 | tf_op jit(solution)/shard_map/reduce_scatter | solution.py:31
  430.5 1.5 convert_element_type.16
  432.0 59.0 %reduce-scatter.11.cloned.1.call-done = f32[32,1024]{1,0:T(8,128)} async-done(((f32[512,1024]{1,0:T(8,128)}), f32[32,1024]{1,0:T(8,128)}) %reduce-scatter.11.cloned.1.call-update) | async-done | bytes 131088 | tf_op jit(solution)/shard_map/reduce_scatter | solution.py:48
  491.0 1.5 convert_element_type.19
Async XLA Ops:
  7.2 45.5 %copy-start = (bf16[1664,1024]{1,0:T(8,128)(2,1)S(1)}, bf16[1664,1024]{1,0:T(8,128)(2,1)}, u32[]{:S(2)}) copy-start(bf16[1664,1024]{1,0:T(8,128)(2,1)} %param.9) | copy-start | bytes 10223620
  7.2 45.5 %all-gather.9.cloned.1.call-start = ((), (), s32[]{:S(2)}) async-start(), calls=%async_computation.8 | async-start | bytes 1114112 | tf_op jit(solution)/shard_map/all_gather | solution.py:34
  7.9 83.9 %all-gather.5.cloned.1.call-start = ((), (), s32[]{:S(2)}) async-start(), calls=%async_computation.4 | async-start | bytes 1114112 | tf_op jit(solution)/shard_map/all_gather | solution.py:15
  8.7 164.6 %reduce-scatter.9.cloned.1.call-start = ((), (), s32[]{:S(2)}) async-start(), calls=%async_computation.9 | async-start | bytes 3620864 | tf_op jit(solution)/shard_map/reduce_scatter | solution.py:36
  57.8 206.3 %reduce-scatter.5.cloned.1.call-start = ((), (), s32[]{:S(2)}) async-start(), calls=%async_computation.5 | async-start | bytes 7241728 | tf_op jit(solution)/shard_map/reduce_scatter | solution.py:19
  91.8 4.5 copy-start.1
  91.8 4.5 copy-start.4
  101.8 213.7 %all-gather.7.cloned.1.call-start = ((), (), s32[]{:S(2)}) async-start(), calls=%async_computation.6 | async-start | bytes 1810432 | tf_op jit(solution)/shard_map/all_gather | solution.py:27
  266.1 106.0 %all-gather.11.cloned.1.call-start = ((), (), s32[]{:S(2)}) async-start(), calls=%async_computation.10 | async-start | bytes 3620864 | tf_op jit(solution)/shard_map/all_gather | solution.py:44
  267.8 162.7 %reduce-scatter.7.cloned.1.call-start = ((), (), s32[]{:S(2)}) async-start(), calls=%async_computation.7 | async-start | bytes 2228224 | tf_op jit(solution)/shard_map/reduce_scatter | solution.py:31
  320.3 170.6 %reduce-scatter.11.cloned.1.call-start = ((), (), s32[]{:S(2)}) async-start(), calls=%async_computation.11 | async-start | bytes 2228224 | tf_op jit(solution)/shard_map/reduce_scatter | solution.py:48
  372.1 4.7 copy-start.2
  372.1 4.7 copy-start.3
Sparse Core Ops, SparseCore 0:
  9.8 42.7 all-gather.8
  54.5 37.2 all-gather.4
  95.4 77.7 reduce-scatter.8
  176.8 87.2 reduce-scatter.4
  266.8 48.6 all-gather.6
  318.1 53.9 all-gather.10
  374.8 55.6 reduce-scatter.6
  433.1 57.7 reduce-scatter.10
where the time goes:
time: 502 us; the launch traced here: 499 us
  waiting for transfers between devices  450 us (90%)
  matrix products  24.7 us (5%)
  between operations  14.2 us (3%)
  other arithmetic  9.94 us (2%)
    reduce_scatter x1, waiting for transfers between devices, body(): lax.psum_scatter(jnp.concatenate((gate_part, up_part), axis=1), 'row', sc...  90.9 us
    reduce_scatter x1, waiting for transfers between devices, body(): lax.psum_scatter(transposed(block, down_weight), 'row', scatter_dimension...  71.4 us
    reduce_scatter x1, waiting for transfers between devices, body(): lax.psum_scatter(grad_terms, 'col', scatter_dimension=0, tiled=True)  59 us
    all_gather x1, waiting for transfers between devices, body(): piece_rows = lax.all_gather(stacked_grads, 'row', axis=0, tiled=True)  51.7 us
    reduce_scatter x1, waiting for transfers between devices, body(): lax.psum_scatter(output_terms, 'col', scatter_dimension=0, tiled=True)  50.2 us
    all_gather x1, waiting for transfers between devices, body(): lax.all_gather(hidden, 'row', axis=0, tiled=True)  47.6 us
    all_gather x1, waiting for transfers between devices, body(): seen_grads = lax.all_gather(cotangent, 'col', axis=0, tiled=True)  44 us
    all_gather x1, waiting for transfers between devices, body(): seen_tokens = lax.all_gather(tokens, 'col', axis=0, tiled=True)  33.9 us
  transfers between devices with their start and end apart: 8, of which 8 were waited for; matrix products, arithmetic and copies ran while one was open for 6% of the time, Pallas kernels for 0%

commit v1 on v0

v1 whole, which is shorter than its diff:
```python
import functools

import jax
import jax.numpy as jnp
from jax import lax
from jax.experimental import pallas as pl
from jax.experimental.pallas import tpu as pltpu
from jax.sharding import PartitionSpec as P

MESH = pl.DeviceIdType.MESH
NX, NY, NZ = 4, 4, 8
NB = NX * NY
HALF = 16
TILE = 256


def kernel(
    split,
    tokens,
    cotangent,
    gate_weight,
    up_weight,
    down_weight,
    output,
    input_grad,
    gu_w,
    down_w,
    seen,
    send1_p,
    send1_q,
    full_p,
    full_q,
    recv1_p,
    recv1_q,
    send2_p,
    send2_q,
    recv2_p,
    recv2_q,
    own2_p,
    own2_q,
    gate_up,
    hidden,
    grads,
    acc,
    pair,
    zsend,
    zrecv,
    load_sem,
    seen_s,
    seen_r,
    share_s,
    share_r,
    rs1_s,
    rs1_r,
    rs2_s,
    rs2_r,
    ag1_s,
    ag1_r,
    ag2_s,
    ag2_r,
    pair_s,
    pair_r,
    z_s,
    z_r,
):
    width = gate_weight.shape[1]
    row, col = lax.axis_index("row"), lax.axis_index("col")
    x, y = row // NY, row % NY
    z, k = col // 2, col % 2

    def at(dx=0, dy=0, dz=0, dk=0):
        return (
            ((x + dx) % NX) * NY + (y + dy) % NY,
            ((z + dz) % NZ) * 2 + (k + dk) % 2,
        )

    def remote(src, dst, send, recv, device):
        return pltpu.make_async_remote_copy(
            src_ref=src,
            dst_ref=dst,
            send_sem=send,
            recv_sem=recv,
            device_id=device,
            device_id_type=MESH,
        )

    offset = (0, split)
    widths = (split, width - split)
    span1 = tuple(pl.ds(offset[o], widths[o]) for o in range(2))
    span2 = tuple(pl.ds(2 * offset[o], 2 * widths[o]) for o in range(2))

    loads = []
    for i, (src, dst) in enumerate(
        [(tokens.at[pl.ds(g * HALF, HALF)], seen.at[0, g, col]) for g in range(2)]
        + [(cotangent.at[pl.ds(g * HALF, HALF)], seen.at[1, g, col]) for g in range(2)]
        + [
            (src.at[:, span1[o]], gu_w.at[:, pl.ds(2 * offset[o] + p * widths[o], widths[o])])
            for o in range(2)
            for p, src in enumerate((gate_weight, up_weight))
        ]
        + [(down_weight, down_w)]
    ):
        loads.append(pltpu.make_async_copy(src, dst, load_sem.at[i]))

    barrier = pltpu.get_barrier_semaphore()
    friends = (
        [at(dx=d) for d in range(1, NX)]
        + [at(dy=d) for d in range(1, NY)]
        + [at(dz=d) for d in range(1, NZ)]
        + [at(dk=1)]
    )
    for friend in friends:
        pl.semaphore_signal(barrier, inc=1, device_id=friend, device_id_type=MESH)
    for load in loads:
        load.start()
    pl.semaphore_wait(barrier, len(friends))

    pending = []

    def go(copy):
        copy.start()
        pending.append(copy)

    def own_block(t, g):
        return (tokens, cotangent)[t].at[pl.ds(g * HALF, HALF)]

    def gather_copies(t, g):
        return [
            remote(
                own_block(t, g),
                seen.at[t, g, col],
                seen_s.at[t, g, d - 1],
                seen_r.at[t, g, d - 1],
                at(dz=d),
            )
            for d in range(1, NZ)
        ]

    def share_copy(t, g, d):
        block = ((z - d) % NZ) * 2 + k
        src = own_block(t, g) if d == 0 else seen.at[t, g, block]
        return remote(
            src, seen.at[t, g, block], share_s.at[t, g, d], share_r.at[t, g, d], at(dk=1)
        )

    def gather_start(t, g):
        order = sorted(range(1, NZ), key=lambda d: -min(d, NZ - d))
        copies = gather_copies(t, g)
        for d in order:
            go(copies[d - 1])
        go(share_copy(t, g, 0))

    def gather_finish(t, g):
        copies = gather_copies(t, g)
        for d in sorted(range(1, NZ), key=lambda d: min(d, NZ - d)):
            copies[d - 1].wait_recv()
            go(share_copy(t, g, d))
        for d in range(NZ):
            share_copy(t, g, d).wait_recv()
        loads[2 * t + g].wait()

    def product(left, weight, turned, full, send, g, start, extent):
        def tile(first, size):
            cols = pl.ds(first, size)
            if turned:
                term = lax.dot_general(
                    left, weight[cols, :], (((1,), (1,)), ((), ())),
                    preferred_element_type=jnp.float32,
                )
            else:
                term = jnp.dot(left, weight[:, cols], preferred_element_type=jnp.float32)
            term = term.reshape(NX, NY, HALF, size)
            full[g, :, :, :, cols] = term
            send[g, :, :, :, cols] = term.astype(jnp.bfloat16)

        count = extent // TILE

        @pl.loop(0, count)
        def _(n):
            tile(pl.multiple_of(start + n * TILE, 128), TILE)

        if extent % TILE:
            tile(start + count * TILE, extent % TILE)

    kinds = (
        (span2, full_p, send1_p, recv1_p, send2_p, recv2_p, own2_p),
        (span1, full_q, send1_q, recv1_q, send2_q, recv2_q, own2_q),
    )

    def rs1_copies(q, g, o):
        span, _, send1, recv1, _, _, _ = kinds[q]
        copies = []
        for d in range(1, NX):
            if o == 0:
                src, device = send1.at[g, (x + d) % NX, :, :, span[o]], at(dx=d)
            else:
                src, device = send1.at[g, :, (y + d) % NY, :, span[o]], at(dy=d)
            copies.append(
                remote(
                    src,
                    recv1.at[g, d - 1, :, :, span[o]],
                    rs1_s.at[q, g, o, d - 1],
                    rs1_r.at[q, g, o, d - 1],
                    device,
                )
            )
        return copies

    def step_b(q, g, o):
        left = seen[q, g].reshape(NB * HALF, seen.shape[-1])
        if q == 0:
            product(left, gu_w, False, full_p, send1_p, g, 2 * offset[o], 2 * widths[o])
        else:
            product(left, down_w, True, full_q, send1_q, g, offset[o], widths[o])
        copies = rs1_copies(q, g, o)
        for d in (2, 1, 3):
            go(copies[d - 1])

    def rs2_copies(q, g, o):
        span, _, _, _, send2, recv2, _ = kinds[q]
        return [
            remote(
                send2.at[g, ((y if o == 0 else x) + d) % NX, :, span[o]],
                recv2.at[g, d - 1, :, span[o]],
                rs2_s.at[q, g, o, d - 1],
                rs2_r.at[q, g, o, d - 1],
                at(dy=d) if o == 0 else at(dx=d),
            )
            for d in range(1, NX)
        ]

    def step_s1(q, g, o):
        span, full, _, recv1, send2, _, own2 = kinds[q]
        for copy in rs1_copies(q, g, o):
            copy.wait_recv()

        def total(i):
            mine = full[g, x, i, :, span[o]] if o == 0 else full[g, i, y, :, span[o]]
            for d in range(NX - 1):
                mine += recv1[g, d, i, :, span[o]].astype(jnp.float32)
            return mine

        for i in range(NX):
            send2[g, i, :, span[o]] = total(i).astype(jnp.bfloat16)
        own2[g, :, span[o]] = total(y if o == 0 else x)
        for copy in rs2_copies(q, g, o):
            go(copy)

    def ag_bufs(q):
        return (hidden, span1) if q == 0 else (grads, span2)

    def ag1_copies(q, g, o):
        buf, span = ag_bufs(q)
        mine = buf.at[g, x, y, :, span[o]]
        return [
            remote(
                mine,
                mine,
                ag1_s.at[q, g, o, d - 1],
                ag1_r.at[q, g, o, d - 1],
                at(dy=d) if o == 0 else at(dx=d),
            )
            for d in range(1, NX)
        ]

    def ag2_copies(q, g, o):
        buf, span = ag_bufs(q)
        mine = buf.at[g, x, :, :, span[o]] if o == 0 else buf.at[g, :, y, :, span[o]]
        return [
            remote(
                mine,
                mine,
                ag2_s.at[q, g, o, d - 1],
                ag2_r.at[q, g, o, d - 1],
                at(dx=d) if o == 0 else at(dy=d),
            )
            for d in range(1, NX)
        ]

    def step_s2(q, g, o):
        span, _, _, _, _, recv2, own2 = kinds[q]
        for copy in rs2_copies(q, g, o):
            copy.wait_recv()
        total = own2[g, :, span[o]]
        for d in range(NX - 1):
            total += recv2[g, d, :, span[o]].astype(jnp.float32)
        first, second = (
            pl.ds(2 * offset[o], widths[o]),
            pl.ds(2 * offset[o] + widths[o], widths[o]),
        )
        if q == 0:
            gate_up[g, :, span[o]] = total
            gate, up = total[:, : widths[o]], total[:, widths[o] :]
            hidden[g, x, y, :, span1[o]] = (gate * jax.nn.sigmoid(gate) * up).astype(
                jnp.bfloat16
            )
        else:
            gate, up = gate_up[g, :, first], gate_up[g, :, second]
            sigmoid = jax.nn.sigmoid(gate)
            grads[g, x, y, :, first] = (
                total * up * sigmoid * (1.0 + gate * (1.0 - sigmoid))
            ).astype(jnp.bfloat16)
            grads[g, x, y, :, second] = (total * gate * sigmoid).astype(jnp.bfloat16)
        for copy in ag1_copies(q, g, o):
            go(copy)

    def step_g1(q, g, o):
        for copy in ag1_copies(q, g, o):
            copy.wait_recv()
        copies = ag2_copies(q, g, o)
        for d in (2, 1, 3):
            go(copies[d - 1])

    def pair_copy(t, g):
        return remote(
            acc.at[t, g, :, 1 - k],
            pair.at[t, g],
            pair_s.at[t, g],
            pair_r.at[t, g],
            at(dk=1),
        )

    def step_f(q, g):
        for o in range(2):
            for copy in ag2_copies(q, g, o):
                copy.wait_recv()
        buf, _ = ag_bufs(q)
        left = buf[g].reshape(NB * HALF, buf.shape[-1])

        @pl.loop(0, down_w.shape[1] // TILE)
        def _(n):
            cols = pl.ds(pl.multiple_of(n * TILE, TILE), TILE)
            if q == 0:
                term = jnp.dot(left, down_w[:, cols], preferred_element_type=jnp.float32)
            else:
                term = lax.dot_general(
                    left, gu_w[cols, :], (((1,), (1,)), ((), ())),
                    preferred_element_type=jnp.float32,
                )
            acc[q, g, :, :, :, cols] = term.reshape(NZ, 2, HALF, TILE)

        go(pair_copy(q, g))

    def z_copies(t, g):
        return [
            remote(
                zsend.at[t, g, (z + d) % NZ],
                zrecv.at[t, g, d - 1],
                z_s.at[t, g, d - 1],
                z_r.at[t, g, d - 1],
                at(dz=d),
            )
            for d in range(1, NZ)
        ]

    def step_z(t, g):
        pair_copy(t, g).wait_recv()

        @pl.loop(0, NZ)
        def _(i):
            zsend[t, g, i] = (acc[t, g, i, k] + pair[t, g, i]).astype(jnp.bfloat16)

        copies = z_copies(t, g)
        for d in sorted(range(1, NZ), key=lambda d: -min(d, NZ - d)):
            go(copies[d - 1])

    def step_out(t, g):
        total = acc[t, g, z, k] + pair[t, g, z]
        for d in range(1, NZ):
            z_copies(t, g)[d - 1].wait_recv()
            total += zrecv[t, g, d - 1].astype(jnp.float32)
        (output, input_grad)[t][pl.ds(g * HALF, HALF), :] = total.astype(jnp.bfloat16)

    def both(step, q, g):
        for o in range(2):
            step(q, g, o)

    gather_start(0, 0)
    gather_finish(0, 0)
    gather_start(0, 1)
    for load in loads[4:8]:
        load.wait()
    both(step_b, 0, 0)
    gather_finish(0, 1)
    gather_start(1, 0)
    both(step_b, 0, 1)
    both(step_s1, 0, 0)
    gather_finish(1, 0)
    gather_start(1, 1)
    loads[8].wait()
    both(step_b, 1, 0)
    both(step_s2, 0, 0)
    both(step_s1, 0, 1)
    gather_finish(1, 1)
    both(step_b, 1, 1)
    both(step_g1, 0, 0)
    both(step_s2, 0, 1)
    both(step_s1, 1, 0)
    step_f(0, 0)
    both(step_g1, 0, 1)
    both(step_s2, 1, 0)
    both(step_s1, 1, 1)
    step_z(0, 0)
    step_f(0, 1)
    both(step_g1, 1, 0)
    both(step_s2, 1, 1)
    step_z(0, 1)
    step_out(0, 0)
    both(step_g1, 1, 1)
    step_f(1, 0)
    step_out(0, 1)
    step_z(1, 0)
    step_f(1, 1)
    step_z(1, 1)
    step_out(1, 0)
    step_out(1, 1)
    for copy in pending:
        copy.wait_send()


def body(tokens, cotangent, gate_weight, up_weight, down_weight):
    rows, depth = tokens.shape
    width = gate_weight.shape[1]
    split = (width // 128 + 1) // 2 * 128
    bf16, f32, dma = jnp.bfloat16, jnp.float32, pltpu.SemaphoreType.DMA
    vmem = pltpu.VMEM
    assert rows == 2 * HALF
    scratch = [
        vmem((depth, 2 * width), bf16),
        vmem((width, depth), bf16),
        vmem((2, 2, 2 * NZ, HALF, depth), bf16),
        vmem((2, NX, NY, HALF, 2 * width), bf16),
        vmem((2, NX, NY, HALF, width), bf16),
        vmem((2, NX, NY, HALF, 2 * width), f32),
        vmem((2, NX, NY, HALF, width), f32),
        vmem((2, NX - 1, NX, HALF, 2 * width), bf16),
        vmem((2, NX - 1, NX, HALF, width), bf16),
        vmem((2, NX, HALF, 2 * width), bf16),
        vmem((2, NX, HALF, width), bf16),
        vmem((2, NX - 1, HALF, 2 * width), bf16),
        vmem((2, NX - 1, HALF, width), bf16),
        vmem((2, HALF, 2 * width), f32),
        vmem((2, HALF, width), f32),
        vmem((2, HALF, 2 * width), f32),
        vmem((2, NX, NY, HALF, width), bf16),
        vmem((2, NX, NY, HALF, 2 * width), bf16),
        vmem((2, 2, NZ, 2, HALF, depth), f32),
        vmem((2, 2, NZ, HALF, depth), f32),
        vmem((2, 2, NZ, HALF, depth), bf16),
        vmem((2, 2, NZ - 1, HALF, depth), bf16),
        dma((9,)),
        dma((2, 2, NZ - 1)),
        dma((2, 2, NZ - 1)),
        dma((2, 2, NZ)),
        dma((2, 2, NZ)),
    ]
    scratch += [dma((2, 2, 2, NX - 1)) for _ in range(8)]
    scratch += [dma((2, 2)), dma((2, 2)), dma((2, 2, NZ - 1)), dma((2, 2, NZ - 1))]
    shape = jax.ShapeDtypeStruct((rows, depth), bf16)
    return pl.pallas_call(
        functools.partial(kernel, split),
        name="swiglu_both_ways",
        out_shape=(shape, shape),
        in_specs=[pl.BlockSpec(memory_space=pl.ANY)] * 5,
        out_specs=(pl.BlockSpec(memory_space=pltpu.VMEM),) * 2,
        scratch_shapes=scratch,
        compiler_params=pltpu.CompilerParams(
            collective_id=0, has_side_effects=True, vmem_limit_bytes=60 << 20
        ),
    )(tokens, cotangent, gate_weight, up_weight, down_weight)


def solution(mesh):
    placed = (P("col", "row"), P("col", "row"), P("row", "col"), P("row", "col"), P("col", "row"))
    return jax.shard_map(
        body,
        mesh=mesh,
        in_specs=placed,
        out_specs=(P("col", "row"), P("col", "row")),
        check_vma=False,
    )
```

time: 502 us -> 121 us (0.24)
  waiting for transfers between devices: 450 us -> 0 us
  Pallas kernels: 0 us -> 118 us
  matrix products: 24.7 us -> 0 us
  between operations: 14.2 us -> 0.64 us
  other arithmetic: 9.94 us -> 0 us
    reduce_scatter x4 -> x0, waiting for transfers between devices: 272 us -> none  [the longest x1 90.9 us: body(): lax.psum_scatter(jnp.concatenate((gate_part, up_part), axis=1), 'row', sc...]
    all_gather x4 -> x0, waiting for transfers between devices: 177 us -> none  [the longest x1 51.7 us: body(): piece_rows = lax.all_gather(stacked_grads, 'row', axis=0, tiled=True)]
    pallas_call x0 -> x1, Pallas kernels: none -> 118 us  [body(): pl.pallas_call(functools.partial(kernel, split), name='swiglu_both_ways',...]
    dot_general x6 -> x0, matrix products: 24.7 us -> none  [the longest x3 13.3 us: transposed(): lax.dot_general(left, right, (((1,), (1,)), ((), ())), preferred_element_...]
  transfers between devices with their start and end apart: 8 -> 0, of which waited for: 8 -> 0; matrix products, arithmetic and copies ran while one was open for 6% -> 0% of each run, Pallas kernels for 0% -> 0%
where the time goes in v1:
time: 121 us
  Pallas kernels  118 us (98%)
  local copies, waits for them, and re-layouts  2.95 us (2%)
    pallas_call x1, Pallas kernels, body(): pl.pallas_call(functools.partial(kernel, split), name='swiglu_both_ways',...  118 us
    unnamed x2, local copies, waits for them, and re-layouts  2.95 us

profile of v1, /device:TPU:1, one launch (start us, length us, event | category | flops | bytes accessed | tf_op | source)
XLA Modules:
  0.0 121.1 jit_solution(12740780592997419647)
XLA Ops:
  0.6 117.6 %swiglu_both_ways.1 = (bf16[32,1024]{1,0:T(8,128)(2,1)}, bf16[32,1024]{1,0:T(8,128)(2,1)}) custom-call(bf16[32,1024]{1,0:T(8,128)(2,1)} %tokens.1, bf16[32,1024]{1,0:T(8,128)(2,1)} %cotangent.1, bf16[1024,1664]{1,0:T(8,128)(2,1)} %gate_weight.1, bf16[1024,1664]{1,0:T(8,128)(2,1)} %up_weight.1, bf16[1664,1024]{1,0:T(8,128)(2,1)} %down_weight.1), custom_call_target="tpu_custom_call" | custom-call | tf_op jit(solution)/shard_map/swiglu_both_ways/pallas_call | solution.py:460
  118.2 1.5 %copy.9 = bf16[32,1024]{1,0:T(8,128)(2,1)} copy(bf16[32,1024]{1,0:T(8,128)(2,1)} %get-tuple-element.4) | data formatting | bytes 131072
  119.7 1.5 %copy.10 = bf16[32,1024]{1,0:T(8,128)(2,1)} copy(bf16[32,1024]{1,0:T(8,128)(2,1)} %get-tuple-element.5) | data formatting | bytes 131072

commit v2 on v1

v2 whole, which is shorter than its diff:
```python
import functools

import jax
import jax.numpy as jnp
from jax import lax
from jax.experimental import pallas as pl
from jax.experimental.pallas import tpu as pltpu
from jax.sharding import PartitionSpec as P

MESH = pl.DeviceIdType.MESH
NX, NY, NZ = 4, 4, 8
NB = NX * NY
HALF = 16
TILE = 256
GROUPS = (
    ((0, 2, -1, 0), (2, 2, 0, 0), (4, 2, 1, 0), (6, 1, 2, 0), (7, 1, -2, 0)),
    ((0, 1, 2, 1), (1, 1, -2, 1), (2, 2, 3, 0), (4, 2, -3, 0), (6, 2, 4, 0)),
)
NEAR, FAR = 0, 1
SEMAPHORES = {
    "seen": (2, 2, 5),
    "share": (2, 2, 5),
    "rs1": (2, 2, 2, 6),
    "rs2": (2, 2, 2, NX - 1),
    "ag1": (2, 2, 2, NX - 1),
    "ag2": (2, 2, 2, 6),
    "pair": (2, 2, 2),
    "z": (2, 2, 2, 5),
}
KINDS = tuple(SEMAPHORES)


def kernel(
    split,
    tokens,
    cotangent,
    gate_weight,
    up_weight,
    down_weight,
    both_out,
    gu_w,
    down_w,
    seen,
    send1_p,
    send1_q,
    full_p,
    full_q,
    recv1_p,
    recv1_q,
    relay_p,
    relay_q,
    send2_p,
    send2_q,
    recv2_p,
    recv2_q,
    own2_p,
    own2_q,
    gate_up,
    hidden,
    grads,
    acc,
    pair,
    zsend,
    zrecv,
    result,
    load_sem,
    *sems,
):
    width = gate_weight.shape[1]
    row, col = lax.axis_index("row"), lax.axis_index("col")
    x, y = row // NY, row % NY
    z, k = col // 2, col % 2

    def at(dx=0, dy=0, dz=0, dk=0):
        return (
            ((x + dx) % NX) * NY + (y + dy) % NY,
            ((z + dz) % NZ) * 2 + (k + dk) % 2,
        )

    def remote(src, dst, kind, index, device):
        send, recv = sems[2 * KINDS.index(kind)], sems[2 * KINDS.index(kind) + 1]
        return pltpu.make_async_remote_copy(
            src_ref=src,
            dst_ref=dst,
            send_sem=send.at[index],
            recv_sem=recv.at[index],
            device_id=device,
            device_id_type=MESH,
        )

    offset = (0, split)
    widths = (split, width - split)
    span1 = tuple(pl.ds(offset[o], widths[o]) for o in range(2))
    span2 = tuple(pl.ds(2 * offset[o], 2 * widths[o]) for o in range(2))

    loads = [
        pltpu.make_async_copy(src, dst, load_sem.at[i])
        for i, (src, dst) in enumerate(
            [(tokens, seen.at[0, NEAR, pl.ds(2, 2), k]), (cotangent, seen.at[1, NEAR, pl.ds(2, 2), k])]
            + [
                (
                    src.at[:, span1[o]],
                    gu_w.at[:, pl.ds(2 * offset[o] + p * widths[o], widths[o])],
                )
                for o in range(2)
                for p, src in enumerate((gate_weight, up_weight))
            ]
            + [(down_weight, down_w)]
        )
    ]

    barrier = pltpu.get_barrier_semaphore()
    friends = (
        [at(dx=d) for d in range(1, NX)]
        + [at(dy=d) for d in range(1, NY)]
        + [at(dz=d) for d in range(1, NZ)]
        + [at(dk=1)]
    )
    for friend in friends:
        pl.semaphore_signal(barrier, inc=1, device_id=friend, device_id_type=MESH)
    pl.semaphore_wait(barrier, len(friends))

    pending = []

    def go(copy):
        copy.start()
        pending.append(copy)

    def own_block(t, n, h):
        return (tokens, cotangent)[t].at[pl.ds(h, n)]

    def gather_copy(t, g, e):
        j, n, dz, h = GROUPS[g][e]
        return remote(
            own_block(t, n, h), seen.at[t, g, pl.ds(j, n), k], "seen", (t, g, e), at(dz=-dz)
        )

    def share_copy(t, g, e):
        j, n, dz, h = GROUPS[g][e]
        block = seen.at[t, g, pl.ds(j, n), k]
        src = own_block(t, n, h) if dz == 0 else block
        return remote(src, block, "share", (t, g, e), at(dk=1))

    def gather_start(t, g):
        for e, (_, _, dz, _) in enumerate(GROUPS[g]):
            go(gather_copy(t, g, e) if dz else share_copy(t, g, e))

    def gather_finish(t, g, then=None):
        runs = sorted(enumerate(GROUPS[g]), key=lambda run: abs(run[1][2]))
        for e, (_, _, dz, _) in runs:
            if dz:
                gather_copy(t, g, e).wait_recv()
                go(share_copy(t, g, e))
        if then is not None:
            gather_start(*then)
        for e, _ in runs:
            share_copy(t, g, e).wait_recv()

    def product(left, weight, turned, full, send, g, start, extent):
        def tile(first, size):
            cols = pl.ds(first, size)
            if turned:
                term = lax.dot_general(
                    left, weight[cols, :], (((1,), (1,)), ((), ())),
                    preferred_element_type=jnp.float32,
                )
            else:
                term = jnp.dot(left, weight[:, cols], preferred_element_type=jnp.float32)
            term = term.reshape(NX, NY, HALF, size)
            full[g, :, :, :, cols] = term
            send[g, :, :, :, cols] = term.astype(jnp.bfloat16)

        count = extent // TILE

        @pl.loop(0, count)
        def _(n):
            tile(pl.multiple_of(start + n * TILE, 128), TILE)

        if extent % TILE:
            tile(start + count * TILE, extent % TILE)

    kinds = (
        (span2, full_p, send1_p, recv1_p, relay_p, send2_p, recv2_p, own2_p),
        (span1, full_q, send1_q, recv1_q, relay_q, send2_q, recv2_q, own2_q),
    )
    low, high, whole = pl.ds(0, NX // 2), pl.ds(NX // 2, NX // 2), pl.ds(0, NX)

    def line(o, step):
        return (at(dx=step), (x + step) % NX) if o == 0 else (at(dy=step), (y + step) % NY)

    def part(buf, g, o, chunk, inner, cols):
        if o == 0:
            return buf.at[g, chunk, inner, :, cols]
        return buf.at[g, inner, chunk, :, cols]

    def rs1_copies(q, g, o):
        span, _, send1, recv1, relay, _, _, _ = kinds[q]
        (right, after), (left, before), (_, opposite) = line(o, 1), line(o, -1), line(o, 2)
        plan = [
            (right, opposite, low, relay.at[g, low, :, span[o]]),
            (left, opposite, high, relay.at[g, high, :, span[o]]),
            (right, after, high, recv1.at[g, 0, high, :, span[o]]),
            (left, before, low, recv1.at[g, 1, low, :, span[o]]),
            (right, after, low, recv1.at[g, 0, low, :, span[o]]),
            (left, before, high, recv1.at[g, 1, high, :, span[o]]),
        ]
        return [
            remote(part(send1, g, o, chunk, inner, span[o]), dst, "rs1", (q, g, o, n), device)
            for n, (device, chunk, inner, dst) in enumerate(plan)
        ]

    def step_b(q, g):
        left = seen[q, g].reshape(NB * HALF, seen.shape[-1])
        for o in range(2):
            if q == 0:
                product(left, gu_w, False, full_p, send1_p, g, 2 * offset[o], 2 * widths[o])
            else:
                product(left, down_w, True, full_q, send1_q, g, offset[o], widths[o])
            for copy in rs1_copies(q, g, o)[:2]:
                go(copy)
        for o in range(2):
            for copy in rs1_copies(q, g, o)[2:4]:
                go(copy)

    def step_r(q, g, o):
        span, full, send1, _, relay, _, _, _ = kinds[q]
        copies = rs1_copies(q, g, o)
        for side, blocks in enumerate((range(NX // 2), range(NX // 2, NX))):
            copies[side].wait_recv()
            _, chunk = line(o, 1 - 2 * side)
            for i in blocks:
                total = part(full, g, o, chunk, i, span[o])[...]
                total += relay[g, i, :, span[o]].astype(jnp.float32)
                part(send1, g, o, chunk, i, span[o])[...] = total.astype(jnp.bfloat16)
            go(copies[4 + side])

    def rs2_copies(q, g, o):
        span, _, _, _, _, send2, recv2, _ = kinds[q]
        return [
            remote(
                send2.at[g, ((y if o == 0 else x) + d) % NX, :, span[o]],
                recv2.at[g, d - 1, :, span[o]],
                "rs2",
                (q, g, o, d - 1),
                at(dy=d) if o == 0 else at(dx=d),
            )
            for d in range(1, NX)
        ]

    def step_s1(q, g, o):
        span, full, _, recv1, _, send2, _, own2 = kinds[q]
        for copy in rs1_copies(q, g, o)[2:]:
            copy.wait_recv()

        def total(i):
            mine = full[g, x, i, :, span[o]] if o == 0 else full[g, i, y, :, span[o]]
            for d in range(2):
                mine += recv1[g, d, i, :, span[o]].astype(jnp.float32)
            return mine

        for i in range(NX):
            send2[g, i, :, span[o]] = total(i).astype(jnp.bfloat16)
        own2[g, :, span[o]] = total(y if o == 0 else x)
        for copy in rs2_copies(q, g, o):
            go(copy)

    def ag_bufs(q):
        return (hidden, span1) if q == 0 else (grads, span2)

    def ag1_copies(q, g, o):
        buf, span = ag_bufs(q)
        mine = buf.at[g, x, y, :, span[o]]
        return [
            remote(
                mine,
                mine,
                "ag1",
                (q, g, o, d - 1),
                at(dy=d) if o == 0 else at(dx=d),
            )
            for d in range(1, NX)
        ]

    def ag2_copies(q, g, o):
        buf, span = ag_bufs(q)
        (right, _), (left, before), (_, mine), (_, after) = (
            line(o, 1),
            line(o, -1),
            line(o, 0),
            line(o, 1),
        )
        plan = [
            (right, mine, low),
            (left, mine, high),
            (right, mine, high),
            (left, mine, low),
            (right, before, low),
            (left, after, high),
        ]
        return [
            remote(
                part(buf, g, o, chunk, inner, span[o]),
                part(buf, g, o, chunk, inner, span[o]),
                "ag2",
                (q, g, o, n),
                device,
            )
            for n, (device, chunk, inner) in enumerate(plan)
        ]

    def step_s2(q, g, o):
        span, _, _, _, _, _, recv2, own2 = kinds[q]
        for copy in rs2_copies(q, g, o):
            copy.wait_recv()
        total = own2[g, :, span[o]]
        for d in range(NX - 1):
            total += recv2[g, d, :, span[o]].astype(jnp.float32)
        first, second = (
            pl.ds(2 * offset[o], widths[o]),
            pl.ds(2 * offset[o] + widths[o], widths[o]),
        )
        if q == 0:
            gate_up[g, :, span[o]] = total
            gate, up = total[:, : widths[o]], total[:, widths[o] :]
            hidden[g, x, y, :, span1[o]] = (gate * jax.nn.sigmoid(gate) * up).astype(
                jnp.bfloat16
            )
        else:
            gate, up = gate_up[g, :, first], gate_up[g, :, second]
            sigmoid = jax.nn.sigmoid(gate)
            grads[g, x, y, :, first] = (
                total * up * sigmoid * (1.0 + gate * (1.0 - sigmoid))
            ).astype(jnp.bfloat16)
            grads[g, x, y, :, second] = (total * gate * sigmoid).astype(jnp.bfloat16)
        for copy in ag1_copies(q, g, o):
            go(copy)

    def step_g1(q, g, o):
        for copy in ag1_copies(q, g, o):
            copy.wait_recv()
        for copy in ag2_copies(q, g, o)[:4]:
            go(copy)

    def step_g2(q, g, o):
        copies = ag2_copies(q, g, o)
        for side in range(2):
            copies[side].wait_recv()
            go(copies[4 + side])

    depth = down_w.shape[1]
    strip = depth // 2

    def strip_of(c):
        return pl.ds(c * strip, strip)

    def pair_copy(t, g, c):
        return remote(
            acc.at[t, g, :, 1 - k, :, strip_of(c)],
            pair.at[t, g, :, :, strip_of(c)],
            "pair",
            (t, g, c),
            at(dk=1),
        )

    def step_f(q, g):
        for o in range(2):
            for copy in ag2_copies(q, g, o)[2:]:
                copy.wait_recv()
        buf, _ = ag_bufs(q)
        left = buf[g].reshape(NB * HALF, buf.shape[-1])
        for c in range(2):

            @pl.loop(0, strip // TILE)
            def _(n):
                cols = pl.ds(pl.multiple_of(c * strip + n * TILE, TILE), TILE)
                if q == 0:
                    term = jnp.dot(left, down_w[:, cols], preferred_element_type=jnp.float32)
                else:
                    term = lax.dot_general(
                        left, gu_w[cols, :], (((1,), (1,)), ((), ())),
                        preferred_element_type=jnp.float32,
                    )
                acc[q, g, :, :, :, cols] = term.reshape(NZ, 2, HALF, TILE)

            go(pair_copy(q, g, c))

    def z_copy(t, g, c, e):
        j, n, dz, _ = GROUPS[g][e]
        runs = pl.ds(j, n)
        return remote(
            zsend.at[t, g, runs, :, strip_of(c)],
            zrecv.at[t, g, runs, :, strip_of(c)],
            "z",
            (t, g, c, e),
            at(dz=dz),
        )

    def step_z(t, g):
        for c in range(2):
            pair_copy(t, g, c).wait_recv()

            @pl.loop(0, NZ)
            def _(i):
                zsend[t, g, i, :, strip_of(c)] = (
                    acc[t, g, i, k, :, strip_of(c)] + pair[t, g, i, :, strip_of(c)]
                ).astype(jnp.bfloat16)

            for e, (_, _, dz, _) in sorted(
                enumerate(GROUPS[g]), key=lambda run: -abs(run[1][2])
            ):
                if dz:
                    go(z_copy(t, g, c, e))

    def step_out(t, g, last):
        for c in range(2):
            cols = strip_of(c)
            total = [None, None]
            for h in range(2):
                if last:
                    total[h] = result[t, h, :, cols]
                if g == NEAR:
                    own = acc[t, g, 2 + h, k, :, cols] + pair[t, g, 2 + h, :, cols]
                    total[h] = own if total[h] is None else total[h] + own
            for e, (j, n, dz, first) in enumerate(GROUPS[g]):
                if dz:
                    z_copy(t, g, c, e).wait_recv()
                    for i in range(n):
                        h = first + i
                        term = zrecv[t, g, j + i, :, cols].astype(jnp.float32)
                        total[h] = term if total[h] is None else total[h] + term
            for h in range(2):
                if last:
                    both_out[t, h, :, cols] = total[h].astype(jnp.bfloat16)
                else:
                    result[t, h, :, cols] = total[h]

    def both(step, q, g):
        for o in range(2):
            step(q, g, o)

    gather_start(0, NEAR)
    for load in loads[:6]:
        load.start()
    gather_finish(0, NEAR, (0, FAR))
    loads[6].start()
    for load in (loads[0], *loads[2:6]):
        load.wait()
    step_b(0, NEAR)
    both(step_r, 0, NEAR)
    gather_finish(0, FAR, (1, FAR))
    step_b(0, FAR)
    both(step_s1, 0, NEAR)
    both(step_r, 0, FAR)
    gather_finish(1, FAR, (1, NEAR))
    loads[6].wait()
    step_b(1, FAR)
    both(step_s2, 0, NEAR)
    both(step_s1, 0, FAR)
    both(step_r, 1, FAR)
    both(step_g1, 0, NEAR)
    gather_finish(1, NEAR)
    loads[1].wait()
    step_b(1, NEAR)
    both(step_s2, 0, FAR)
    both(step_g2, 0, NEAR)
    both(step_s1, 1, FAR)
    both(step_r, 1, NEAR)
    both(step_g1, 0, FAR)
    both(step_s2, 1, FAR)
    step_f(0, NEAR)
    both(step_g2, 0, FAR)
    both(step_s1, 1, NEAR)
    both(step_g1, 1, FAR)
    step_z(0, NEAR)
    step_f(0, FAR)
    both(step_s2, 1, NEAR)
    both(step_g2, 1, FAR)
    step_z(0, FAR)
    both(step_g1, 1, NEAR)
    step_f(1, FAR)
    step_out(0, NEAR, False)
    both(step_g2, 1, NEAR)
    step_z(1, FAR)
    step_out(0, FAR, True)
    step_f(1, NEAR)
    step_out(1, FAR, False)
    step_z(1, NEAR)
    step_out(1, NEAR, True)
    for copy in pending:
        copy.wait_send()


def finish(both_out, output, input_grad):
    output[...] = both_out[0]
    input_grad[...] = both_out[1]


def body(tokens, cotangent, gate_weight, up_weight, down_weight):
    rows, depth = tokens.shape
    width = gate_weight.shape[1]
    split = (width // 128 + 1) // 2 * 128
    bf16, f32, dma = jnp.bfloat16, jnp.float32, pltpu.SemaphoreType.DMA
    vmem = pltpu.VMEM
    assert rows == 2 * HALF
    scratch = [
        vmem((depth, 2 * width), bf16),
        vmem((width, depth), bf16),
        vmem((2, 2, NZ, 2, HALF, depth), bf16),
        vmem((2, NX, NY, HALF, 2 * width), bf16),
        vmem((2, NX, NY, HALF, width), bf16),
        vmem((2, NX, NY, HALF, 2 * width), f32),
        vmem((2, NX, NY, HALF, width), f32),
        vmem((2, 2, NX, HALF, 2 * width), bf16),
        vmem((2, 2, NX, HALF, width), bf16),
        vmem((2, NX, HALF, 2 * width), bf16),
        vmem((2, NX, HALF, width), bf16),
        vmem((2, NX, HALF, 2 * width), bf16),
        vmem((2, NX, HALF, width), bf16),
        vmem((2, NX - 1, HALF, 2 * width), bf16),
        vmem((2, NX - 1, HALF, width), bf16),
        vmem((2, HALF, 2 * width), f32),
        vmem((2, HALF, width), f32),
        vmem((2, HALF, 2 * width), f32),
        vmem((2, NX, NY, HALF, width), bf16),
        vmem((2, NX, NY, HALF, 2 * width), bf16),
        vmem((2, 2, NZ, 2, HALF, depth), f32),
        vmem((2, 2, NZ, HALF, depth), f32),
        vmem((2, 2, NZ, HALF, depth), bf16),
        vmem((2, 2, NZ, HALF, depth), bf16),
        vmem((2, 2, HALF, depth), f32),
        dma((7,)),
    ]
    scratch += [dma(SEMAPHORES[kind]) for kind in KINDS for _ in range(2)]
    both_out = pl.pallas_call(
        functools.partial(kernel, split),
        name="swiglu_both_ways",
        out_shape=jax.ShapeDtypeStruct((2, 2, HALF, depth), bf16),
        in_specs=[pl.BlockSpec(memory_space=pl.ANY)] * 5,
        out_specs=pl.BlockSpec(memory_space=pltpu.VMEM),
        scratch_shapes=scratch,
        compiler_params=pltpu.CompilerParams(
            collective_id=0, has_side_effects=True, vmem_limit_bytes=60 << 20
        ),
    )(
        tokens.reshape(2, HALF, depth),
        cotangent.reshape(2, HALF, depth),
        gate_weight,
        up_weight,
        down_weight,
    )
    shape = jax.ShapeDtypeStruct((rows, depth), bf16)
    return pl.pallas_call(
        finish,
        name="finish",
        out_shape=(shape, shape),
        in_specs=[pl.BlockSpec(memory_space=pltpu.VMEM)],
        out_specs=(pl.BlockSpec(memory_space=pltpu.VMEM),) * 2,
    )(both_out.reshape(2, rows, depth))


def solution(mesh):
    placed = (P("col", "row"), P("col", "row"), P("row", "col"), P("row", "col"), P("col", "row"))
    return jax.shard_map(
        body,
        mesh=mesh,
        in_specs=placed,
        out_specs=(P("col", "row"), P("col", "row")),
        check_vma=False,
    )
```

time: 121 us -> 105 us (0.87)
  Pallas kernels: 118 us -> 104 us
  local copies, waits for them, and re-layouts: 2.95 us -> 0 us
    pallas_call x1, Pallas kernels: 118 us -> 103 us  [body(): pl.pallas_call(functools.partial(kernel, split), name='swiglu_both_ways',...]
    unnamed x2 -> x0, local copies, waits for them, and re-layouts: 2.95 us -> none
    pallas_call x0 -> x1, Pallas kernels: none -> 1.56 us  [body(): pl.pallas_call(finish, name='finish', out_shape=(shape, shape), in_specs=...]
where the time goes in v2:
time: 105 us
  Pallas kernels  104 us (99%)
    pallas_call x1, Pallas kernels, body(): pl.pallas_call(functools.partial(kernel, split), name='swiglu_both_ways',...  103 us

profile of v2, /device:TPU:1, one launch (start us, length us, event | category | flops | bytes accessed | tf_op | source)
XLA Modules:
  0.0 104.8 jit_solution(5086387642804352377)
XLA Ops:
  0.6 102.6 %swiglu_both_ways.1 = bf16[2,2,16,1024]{3,2,1,0:T(8,128)(2,1)} custom-call(bf16[2,16,1024]{2,1,0:T(8,128)(2,1)} %bitcast.4, bf16[2,16,1024]{2,1,0:T(8,128)(2,1)} %bitcast.5, bf16[1024,1664]{1,0:T(8,128)(2,1)} %gate_weight.1, bf16[1024,1664]{1,0:T(8,128)(2,1)} %up_weight.1, bf16[1664,1024]{1,0:T(8,128)(2,1)} %down_weight.1), custom_call_target="tpu_custom_call" | custom-call | tf_op jit(solution)/shard_map/swiglu_both_ways/pallas_call | solution.py:534
  103.3 1.6 %finish.1 = (bf16[32,1024]{1,0:T(8,128)(2,1)}, bf16[32,1024]{1,0:T(8,128)(2,1)}) custom-call(bf16[2,32,1024]{2,1,0:T(8,128)(2,1)} %bitcast.3), custom_call_target="tpu_custom_call" | custom-call | tf_op jit(solution)/shard_map/finish/pallas_call | solution.py:552

commit v3 on v2

v3 whole, which is shorter than its diff:
```python
import functools

import jax
import jax.numpy as jnp
from jax import lax
from jax.experimental import pallas as pl
from jax.experimental.pallas import tpu as pltpu
from jax.sharding import PartitionSpec as P

MESH = pl.DeviceIdType.MESH
NX, NY, NZ = 4, 4, 8
NB = NX * NY
HALF = 16
TILE = 256
GROUPS = (
    ((0, 2, 0, 0), (2, 2, -1, 0), (4, 2, 1, 0), (6, 1, 2, 0), (7, 1, -2, 0)),
    ((0, 1, 2, 1), (1, 1, -2, 1), (2, 2, 3, 0), (4, 2, -3, 0), (6, 2, 4, 0)),
)
NEAR, FAR = 0, 1
OTHERS = (pl.ds(2, 6), pl.ds(0, 8))
ARRIVALS = {
    "seen": (2, 2),
    "share": (2, 2),
    "relay": (2, 2, 2),
    "rs1": (2, 2, 2),
    "rs2": (2, 2, 2),
    "ag1": (2, 2, 2),
    "first": (2, 2, 2),
    "rest": (2, 2, 2),
    "pair": (2, 2, 2),
    "z": (2, 2, 2),
}
KINDS = tuple(ARRIVALS)
DEPARTURES = {kind: (2, 2) if kind in ("seen", "share", "z") else (2,) for kind in KINDS}
LAST = (0, 0)
STRIPS = ((2, 2), (2, 2))
SCHEDULE = (
    ("gs", 0, 0), ("gs", 0, 1), ("gw", 0, 0), ("gs", 1, 1), ("b", 0, 0, 1), ("b", 0, 0, 0),
    ("b2", 0, 0, 1), ("r", 0, 0, 1), ("b2", 0, 0, 0), ("gw", 0, 1), ("r", 0, 0, 0),
    ("b", 0, 1, 0), ("s1", 0, 0, 1), ("gs", 1, 0), ("b2", 0, 1, 0), ("b", 0, 1, 1),
    ("s1", 0, 0, 0), ("gw", 1, 1), ("b2", 0, 1, 1), ("s2", 0, 0, 1), ("r", 0, 1, 0),
    ("b", 1, 1, 1), ("gw", 1, 0), ("b", 1, 1, 0), ("r", 0, 1, 1), ("b", 1, 0, 0),
    ("s2", 0, 0, 0), ("g1", 0, 0, 1), ("s1", 0, 1, 0), ("b2", 1, 1, 1), ("r", 1, 1, 1),
    ("r", 1, 1, 0), ("b2", 1, 1, 0), ("b", 1, 0, 1), ("g1", 0, 0, 0), ("s1", 0, 1, 1),
    ("b2", 1, 0, 1), ("s2", 0, 1, 0), ("s1", 1, 1, 0), ("b2", 1, 0, 0), ("g2", 0, 0, 1),
    ("r", 1, 0, 0), ("r", 1, 0, 1), ("s1", 1, 1, 1), ("s2", 0, 1, 1), ("g2", 0, 0, 0),
    ("g1", 0, 1, 0), ("s2", 1, 1, 0), ("s2", 1, 1, 1), ("s1", 1, 0, 0), ("g1", 0, 1, 1),
    ("s1", 1, 0, 1), ("f", 0, 0, 1), ("g2", 0, 1, 0), ("g1", 1, 1, 0), ("g2", 0, 1, 1),
    ("g1", 1, 1, 1), ("f", 0, 0, 0), ("z", 0, 0, 1), ("s2", 1, 0, 1), ("s2", 1, 0, 0),
    ("f", 0, 1, 1), ("g2", 1, 1, 0), ("z", 0, 0, 0), ("z", 0, 1, 1), ("g2", 1, 1, 1),
    ("f", 0, 1, 0), ("z", 0, 1, 0), ("g1", 1, 0, 0), ("g1", 1, 0, 1), ("f", 1, 1, 0),
    ("g2", 1, 0, 0), ("g2", 1, 0, 1), ("out", 0, 1, 1), ("z", 1, 1, 0), ("f", 1, 1, 1),
    ("z", 1, 1, 1), ("f", 1, 0, 1), ("f", 1, 0, 0), ("out", 0, 1, 0), ("z", 1, 0, 1),
    ("out", 0, 0, 1), ("z", 1, 0, 0), ("out", 1, 1, 0), ("out", 1, 1, 1), ("out", 0, 0, 0),
    ("out", 1, 0, 1), ("out", 1, 0, 0),
)


def kernel(
    split,
    tokens,
    cotangent,
    gate_weight,
    up_weight,
    down_weight,
    both_out,
    gu_w,
    down_w,
    seen,
    send1_p,
    send1_q,
    full_p,
    full_q,
    recv1_p,
    recv1_q,
    relay_p,
    relay_q,
    send2_p,
    send2_q,
    recv2_p,
    recv2_q,
    own2_p,
    own2_q,
    gate_up,
    hidden,
    grads,
    acc,
    pair,
    zsend,
    zrecv,
    result,
    load_sem,
    *sems,
):
    width = gate_weight.shape[1]
    row, col = lax.axis_index("row"), lax.axis_index("col")
    x, y = row // NY, row % NY
    z, k = col // 2, col % 2

    def at(dx=0, dy=0, dz=0, dk=0):
        return (
            ((x + dx) % NX) * NY + (y + dy) % NY,
            ((z + dz) % NZ) * 2 + (k + dk) % 2,
        )

    def remote(src, dst, kind, index, device):
        send, recv = sems[2 * KINDS.index(kind)], sems[2 * KINDS.index(kind) + 1]
        return pltpu.make_async_remote_copy(
            src_ref=src,
            dst_ref=dst,
            send_sem=send.at[index[: len(DEPARTURES[kind])]],
            recv_sem=recv.at[index],
            device_id=device,
            device_id_type=MESH,
        )

    def arrive(like, kind, index):
        remote(like, like, kind, index, at(dk=1)).wait_recv()

    def depart(like, kind, index):
        index = (*index, 0, 0)[: len(ARRIVALS[kind])]
        remote(like, like, kind, index, at(dk=1)).wait_send()

    offset = (0, split)
    widths = (split, width - split)
    span1 = tuple(pl.ds(offset[o], widths[o]) for o in range(2))
    span2 = tuple(pl.ds(2 * offset[o], 2 * widths[o]) for o in range(2))

    loads = [
        pltpu.make_async_copy(src, dst, load_sem.at[i])
        for i, (src, dst) in enumerate(
            [(tokens, seen.at[0, NEAR, pl.ds(0, 2), k]), (cotangent, seen.at[1, NEAR, pl.ds(0, 2), k])]
            + [
                (
                    src.at[:, span1[o]],
                    gu_w.at[:, pl.ds(2 * offset[o] + p * widths[o], widths[o])],
                )
                for o in range(2)
                for p, src in enumerate((gate_weight, up_weight))
            ]
            + [(down_weight, down_w)]
        )
    ]

    barrier = pltpu.get_barrier_semaphore()
    friends = (
        [at(dx=d) for d in range(1, NX)]
        + [at(dy=d) for d in range(1, NY)]
        + [at(dz=d) for d in range(1, NZ)]
        + [at(dk=1)]
    )
    for friend in friends:
        pl.semaphore_signal(barrier, inc=1, device_id=friend, device_id_type=MESH)
    for load in loads:
        load.start()
    pl.semaphore_wait(barrier, len(friends))

    def go(copy):
        copy.start()

    def own_block(t, n, h):
        return (tokens, cotangent)[t].at[pl.ds(h, n)]

    def step_gs(t, g):
        for j, n, dz, h in GROUPS[g]:
            block = seen.at[t, g, pl.ds(j, n), k]
            if dz:
                go(remote(own_block(t, n, h), block, "seen", (t, g), at(dz=-dz)))
        if g == NEAR:
            own = seen.at[t, g, pl.ds(0, 2), k]
            go(remote(own_block(t, 2, 0), own, "share", (t, g), at(dk=1)))

    def step_gw(t, g):
        block = seen.at[t, g, OTHERS[g], k]
        arrive(block, "seen", (t, g))
        go(remote(block, block, "share", (t, g), at(dk=1)))

    def product(left, weight, turned, full, send, g, start, extent):
        def tile(first, size):
            cols = pl.ds(first, size)
            if turned:
                term = lax.dot_general(
                    left, weight[cols, :], (((1,), (1,)), ((), ())),
                    preferred_element_type=jnp.float32,
                )
            else:
                term = jnp.dot(left, weight[:, cols], preferred_element_type=jnp.float32)
            term = term.reshape(NX, NY, HALF, size)
            full[g, :, :, :, cols] = term
            send[g, :, :, :, cols] = term.astype(jnp.bfloat16)

        count = extent // TILE

        @pl.loop(0, count)
        def _(n):
            tile(pl.multiple_of(start + n * TILE, 128), TILE)

        if extent % TILE:
            tile(start + count * TILE, extent % TILE)

    kinds = (
        (span2, full_p, send1_p, recv1_p, relay_p, send2_p, recv2_p, own2_p),
        (span1, full_q, send1_q, recv1_q, relay_q, send2_q, recv2_q, own2_q),
    )
    low, high, whole = pl.ds(0, NX // 2), pl.ds(NX // 2, NX // 2), pl.ds(0, NX)

    def along_x(g, o):
        return (g + o) % 2 == 0

    def line(g, o, step):
        if along_x(g, o):
            return at(dx=step), (x + step) % NX
        return at(dy=step), (y + step) % NY

    def cross(g, o, step):
        return line(g + 1, o, step)

    def part(buf, g, o, chunk, inner, cols):
        if along_x(g, o):
            return buf.at[g, chunk, inner, :, cols]
        return buf.at[g, inner, chunk, :, cols]

    def rs1_copies(q, g, o):
        span, _, send1, recv1, relay, _, _, _ = kinds[q]
        (right, after), (left, before) = line(g, o, 1), line(g, o, -1)
        _, opposite = line(g, o, 2)
        plan = [
            ("relay", right, opposite, low, relay.at[g, low, :, span[o]]),
            ("relay", left, opposite, high, relay.at[g, high, :, span[o]]),
            ("rs1", right, after, high, recv1.at[g, 0, high, :, span[o]]),
            ("rs1", left, before, low, recv1.at[g, 1, low, :, span[o]]),
            ("rs1", right, after, low, recv1.at[g, 0, low, :, span[o]]),
            ("rs1", left, before, high, recv1.at[g, 1, high, :, span[o]]),
        ]
        return [
            remote(part(send1, g, o, chunk, inner, span[o]), dst, kind, (q, g, o), device)
            for kind, device, chunk, inner, dst in plan
        ]

    arrived = set()

    def once(key, wait):
        if key not in arrived:
            arrived.add(key)
            wait()

    def tokens_there(q, g):
        arrive(seen.at[q, g, :, k], "share", (q, g))
        if g == NEAR:
            loads[q].wait()

    def step_b(q, g, o):
        once(("seen", q, g), lambda: tokens_there(q, g))
        for n in (6,) if q else (2, 3, 4, 5):
            once(("load", n), loads[n].wait)
        left = seen[q, g].reshape(NB * HALF, seen.shape[-1])
        if q == 0:
            product(left, gu_w, False, full_p, send1_p, g, 2 * offset[o], 2 * widths[o])
        else:
            product(left, down_w, True, full_q, send1_q, g, offset[o], widths[o])
        for copy in rs1_copies(q, g, o)[:2]:
            go(copy)

    def step_b2(q, g, o):
        for copy in rs1_copies(q, g, o)[2:4]:
            go(copy)

    def step_r(q, g, o):
        span, full, send1, _, relay, _, _, _ = kinds[q]
        copies = rs1_copies(q, g, o)
        arrive(relay.at[g, :, :, span[o]], "relay", (q, g, o))
        for side, blocks in enumerate((range(NX // 2), range(NX // 2, NX))):
            _, chunk = line(g, o, 1 - 2 * side)
            for i in blocks:
                total = part(full, g, o, chunk, i, span[o])[...]
                total += relay[g, i, :, span[o]].astype(jnp.float32)
                part(send1, g, o, chunk, i, span[o])[...] = total.astype(jnp.bfloat16)
            go(copies[side - 2])

    def rs2_copies(q, g, o):
        span, _, _, _, _, send2, recv2, _ = kinds[q]
        return [
            remote(
                send2.at[g, cross(g, o, d)[1], :, span[o]],
                recv2.at[g, d - 1, :, span[o]],
                "rs2",
                (q, g, o),
                cross(g, o, d)[0],
            )
            for d in range(1, NX)
        ]

    def step_s1(q, g, o):
        span, full, _, recv1, _, send2, _, own2 = kinds[q]
        arrive(recv1.at[g, :, :, :, span[o]], "rs1", (q, g, o))

        def total(i):
            mine = part(full, g, o, line(g, o, 0)[1], i, span[o])[...]
            for d in range(2):
                mine += recv1[g, d, i, :, span[o]].astype(jnp.float32)
            return mine

        for i in range(NX):
            send2[g, i, :, span[o]] = total(i).astype(jnp.bfloat16)
        own2[g, :, span[o]] = total(cross(g, o, 0)[1])
        for copy in rs2_copies(q, g, o):
            go(copy)

    def ag_bufs(q):
        return (hidden, span1) if q == 0 else (grads, span2)

    def ag1_copies(q, g, o):
        buf, span = ag_bufs(q)
        mine = buf.at[g, x, y, :, span[o]]
        return [
            remote(
                mine,
                mine,
                "ag1",
                (q, g, o),
                cross(g, o, d)[0],
            )
            for d in range(1, NX)
        ]

    def ag2_copies(q, g, o):
        buf, span = ag_bufs(q)
        (right, after), (left, before) = line(g, o, 1), line(g, o, -1)
        _, mine = line(g, o, 0)
        plan = [
            ("first", right, mine, low),
            ("first", left, mine, high),
            ("rest", right, mine, high),
            ("rest", left, mine, low),
            ("rest", right, before, low),
            ("rest", left, after, high),
        ]
        return [
            remote(
                part(buf, g, o, chunk, inner, span[o]),
                part(buf, g, o, chunk, inner, span[o]),
                kind,
                (q, g, o),
                device,
            )
            for kind, device, chunk, inner in plan
        ]

    def step_s2(q, g, o):
        span, _, _, _, _, _, recv2, own2 = kinds[q]
        arrive(recv2.at[g, :, :, span[o]], "rs2", (q, g, o))
        total = own2[g, :, span[o]]
        for d in range(NX - 1):
            total += recv2[g, d, :, span[o]].astype(jnp.float32)
        first, second = (
            pl.ds(2 * offset[o], widths[o]),
            pl.ds(2 * offset[o] + widths[o], widths[o]),
        )
        if q == 0:
            gate_up[g, :, span[o]] = total
            gate, up = total[:, : widths[o]], total[:, widths[o] :]
            hidden[g, x, y, :, span1[o]] = (gate * jax.nn.sigmoid(gate) * up).astype(
                jnp.bfloat16
            )
        else:
            gate, up = gate_up[g, :, first], gate_up[g, :, second]
            sigmoid = jax.nn.sigmoid(gate)
            grads[g, x, y, :, first] = (
                total * up * sigmoid * (1.0 + gate * (1.0 - sigmoid))
            ).astype(jnp.bfloat16)
            grads[g, x, y, :, second] = (total * gate * sigmoid).astype(jnp.bfloat16)
        for copy in ag1_copies(q, g, o):
            go(copy)

    def step_g1(q, g, o):
        buf, span = ag_bufs(q)
        arrive(buf.at[g, 0, pl.ds(0, NX - 1), :, span[o]], "ag1", (q, g, o))
        for copy in ag2_copies(q, g, o)[:4]:
            go(copy)

    def step_g2(q, g, o):
        buf, span = ag_bufs(q)
        arrive(buf.at[g, 0, :, :, span[o]], "first", (q, g, o))
        for copy in ag2_copies(q, g, o)[4:]:
            go(copy)

    depth = down_w.shape[1]

    def strip_of(q, g, c):
        size = depth // STRIPS[q][g]
        return pl.ds(c * size, size)

    def pair_copy(t, g, c):
        return remote(
            acc.at[t, g, :, 1 - k, :, strip_of(t, g, c)],
            pair.at[t, g, :, :, strip_of(t, g, c)],
            "pair",
            (t, g, c),
            at(dk=1),
        )

    def rows_there(q, g):
        buf, span = ag_bufs(q)
        for o in range(2):
            arrive(buf.at[g, pl.ds(0, 2), :, :, span[o]], "rest", (q, g, o))

    def step_f(q, g, c):
        once(("rows", q, g), lambda: rows_there(q, g))
        buf, _ = ag_bufs(q)
        left = buf[g].reshape(NB * HALF, buf.shape[-1])

        strip = strip_of(q, g, c)

        @pl.loop(0, strip.size // TILE)
        def _(n):
            cols = pl.ds(pl.multiple_of(strip.start + n * TILE, TILE), TILE)
            if q == 0:
                term = jnp.dot(left, down_w[:, cols], preferred_element_type=jnp.float32)
            else:
                term = lax.dot_general(
                    left, gu_w[cols, :], (((1,), (1,)), ((), ())),
                    preferred_element_type=jnp.float32,
                )
            acc[q, g, :, :, :, cols] = term.reshape(NZ, 2, HALF, TILE)

        go(pair_copy(q, g, c))

    def z_copy(t, g, c, e):
        j, n, dz, _ = GROUPS[g][e]
        runs = pl.ds(j, n)
        return remote(
            zsend.at[t, g, runs, :, strip_of(t, g, c)],
            zrecv.at[t, g, runs, :, strip_of(t, g, c)],
            "z",
            (t, g, c),
            at(dz=dz),
        )

    def step_z(t, g, c):
        pair_copy(t, g, c).wait_recv()

        @pl.loop(0, NZ)
        def _(i):
            zsend[t, g, i, :, strip_of(t, g, c)] = (
                acc[t, g, i, k, :, strip_of(t, g, c)] + pair[t, g, i, :, strip_of(t, g, c)]
            ).astype(jnp.bfloat16)

        for e, (_, _, dz, _) in sorted(enumerate(GROUPS[g]), key=lambda run: -abs(run[1][2])):
            if dz:
                go(z_copy(t, g, c, e))

    def step_out(t, g, c):
        cols = strip_of(t, g, c)
        last = g == LAST[t]
        total = [result[t, h, :, cols] if last else None for h in range(2)]
        if g == NEAR:
            for h in range(2):
                own = acc[t, g, h, k, :, cols] + pair[t, g, h, :, cols]
                total[h] = own if total[h] is None else total[h] + own
        arrive(zrecv.at[t, g, OTHERS[g], :, cols], "z", (t, g, c))
        for j, n, dz, first in GROUPS[g]:
            if dz:
                for i in range(n):
                    h = first + i
                    term = zrecv[t, g, j + i, :, cols].astype(jnp.float32)
                    total[h] = term if total[h] is None else total[h] + term
        for h in range(2):
            if last:
                both_out[t, h, :, cols] = total[h].astype(jnp.bfloat16)
            else:
                result[t, h, :, cols] = total[h]

    steps = {
        "gs": step_gs,
        "gw": step_gw,
        "b": step_b,
        "b2": step_b2,
        "r": step_r,
        "s1": step_s1,
        "s2": step_s2,
        "g1": step_g1,
        "g2": step_g2,
        "f": step_f,
        "z": step_z,
        "out": step_out,
    }
    for step, *where in SCHEDULE:
        steps[step](*where)

    for q in range(2):
        _, _, _, recv1, relay, _, recv2, _ = kinds[q]
        buf, _ = ag_bufs(q)
        for g in range(2):
            depart(seen.at[q, g, OTHERS[g], k], "seen", (q, g))
            depart(seen.at[q, g, :, k], "share", (q, g))
            depart(zrecv.at[q, g, OTHERS[g]], "z", (q, g))
        depart(relay, "relay", (q,))
        depart(recv1, "rs1", (q,))
        depart(recv2, "rs2", (q,))
        depart(buf.at[:, 0, pl.ds(0, NX - 1)], "ag1", (q,))
        depart(buf.at[:, 0], "first", (q,))
        depart(buf.at[:, pl.ds(0, 2)], "rest", (q,))
        depart(pair.at[q], "pair", (q,))


def finish(both_out, output, input_grad):
    output[...] = both_out[0]
    input_grad[...] = both_out[1]


def body(tokens, cotangent, gate_weight, up_weight, down_weight):
    rows, depth = tokens.shape
    width = gate_weight.shape[1]
    split = (width // 128 + 1) // 2 * 128
    bf16, f32, dma = jnp.bfloat16, jnp.float32, pltpu.SemaphoreType.DMA
    vmem = pltpu.VMEM
    assert rows == 2 * HALF
    scratch = [
        vmem((depth, 2 * width), bf16),
        vmem((width, depth), bf16),
        vmem((2, 2, NZ, 2, HALF, depth), bf16),
        vmem((2, NX, NY, HALF, 2 * width), bf16),
        vmem((2, NX, NY, HALF, width), bf16),
        vmem((2, NX, NY, HALF, 2 * width), f32),
        vmem((2, NX, NY, HALF, width), f32),
        vmem((2, 2, NX, HALF, 2 * width), bf16),
        vmem((2, 2, NX, HALF, width), bf16),
        vmem((2, NX, HALF, 2 * width), bf16),
        vmem((2, NX, HALF, width), bf16),
        vmem((2, NX, HALF, 2 * width), bf16),
        vmem((2, NX, HALF, width), bf16),
        vmem((2, NX - 1, HALF, 2 * width), bf16),
        vmem((2, NX - 1, HALF, width), bf16),
        vmem((2, HALF, 2 * width), f32),
        vmem((2, HALF, width), f32),
        vmem((2, HALF, 2 * width), f32),
        vmem((2, NX, NY, HALF, width), bf16),
        vmem((2, NX, NY, HALF, 2 * width), bf16),
        vmem((2, 2, NZ, 2, HALF, depth), f32),
        vmem((2, 2, NZ, HALF, depth), f32),
        vmem((2, 2, NZ, HALF, depth), bf16),
        vmem((2, 2, NZ, HALF, depth), bf16),
        vmem((2, 2, HALF, depth), f32),
        dma((7,)),
    ]
    scratch += [dma(shapes[kind]) for kind in KINDS for shapes in (DEPARTURES, ARRIVALS)]
    both_out = pl.pallas_call(
        functools.partial(kernel, split),
        name="swiglu_both_ways",
        out_shape=jax.ShapeDtypeStruct((2, 2, HALF, depth), bf16),
        in_specs=[pl.BlockSpec(memory_space=pl.ANY)] * 5,
        out_specs=pl.BlockSpec(memory_space=pltpu.VMEM),
        scratch_shapes=scratch,
        compiler_params=pltpu.CompilerParams(
            collective_id=0, has_side_effects=True, vmem_limit_bytes=60 << 20
        ),
    )(
        tokens.reshape(2, HALF, depth),
        cotangent.reshape(2, HALF, depth),
        gate_weight,
        up_weight,
        down_weight,
    )
    shape = jax.ShapeDtypeStruct((rows, depth), bf16)
    return pl.pallas_call(
        finish,
        name="finish",
        out_shape=(shape, shape),
        in_specs=[pl.BlockSpec(memory_space=pltpu.VMEM)],
        out_specs=(pl.BlockSpec(memory_space=pltpu.VMEM),) * 2,
    )(both_out.reshape(2, rows, depth))


def solution(mesh):
    placed = (P("col", "row"), P("col", "row"), P("row", "col"), P("row", "col"), P("col", "row"))
    return jax.shard_map(
        body,
        mesh=mesh,
        in_specs=placed,
        out_specs=(P("col", "row"), P("col", "row")),
        check_vma=False,
    )
```

time: 105 us -> 96.7 us (0.921)
  Pallas kernels: 104 us -> 96 us
    pallas_call x1, Pallas kernels: 103 us -> 94.4 us  [body(): pl.pallas_call(functools.partial(kernel, split), name='swiglu_both_ways',...]
where the time goes in v3:
time: 96.7 us; the launch traced here: 96.6 us
  Pallas kernels  96 us (99%)
    pallas_call x1, Pallas kernels, body(): pl.pallas_call(functools.partial(kernel, split), name='swiglu_both_ways',...  94.4 us

profile of v3, /device:TPU:1, one launch (start us, length us, event | category | flops | bytes accessed | tf_op | source)
XLA Modules:
  0.0 96.6 jit_solution(17446367067365369049)
XLA Ops:
  0.6 94.4 %swiglu_both_ways.1 = bf16[2,2,16,1024]{3,2,1,0:T(8,128)(2,1)} custom-call(bf16[2,16,1024]{2,1,0:T(8,128)(2,1)} %bitcast.4, bf16[2,16,1024]{2,1,0:T(8,128)(2,1)} %bitcast.5, bf16[1024,1664]{1,0:T(8,128)(2,1)} %gate_weight.1, bf16[1024,1664]{1,0:T(8,128)(2,1)} %up_weight.1, bf16[1664,1024]{1,0:T(8,128)(2,1)} %down_weight.1), custom_call_target="tpu_custom_call" | custom-call | tf_op jit(solution)/shard_map/swiglu_both_ways/pallas_call | solution.py:547
  95.1 1.6 %finish.1 = (bf16[32,1024]{1,0:T(8,128)(2,1)}, bf16[32,1024]{1,0:T(8,128)(2,1)}) custom-call(bf16[2,32,1024]{2,1,0:T(8,128)(2,1)} %bitcast.3), custom_call_target="tpu_custom_call" | custom-call | tf_op jit(solution)/shard_map/finish/pallas_call | solution.py:565

commit v4 on v3

--- a/solution.py
+++ b/solution.py
@@ -25,6 +25,7 @@
     "rs1": (2, 2, 2),
     "rs2": (2, 2, 2),
     "ag1": (2, 2, 2),
+    "ag1on": (2, 2, 2),
     "first": (2, 2, 2),
     "rest": (2, 2, 2),
     "pair": (2, 2, 2),
@@ -35,24 +36,29 @@
 LAST = (0, 0)
 STRIPS = ((2, 2), (2, 2))
 SCHEDULE = (
-    ("gs", 0, 0), ("gs", 0, 1), ("gw", 0, 0), ("gs", 1, 1), ("b", 0, 0, 1), ("b", 0, 0, 0),
-    ("b2", 0, 0, 1), ("r", 0, 0, 1), ("b2", 0, 0, 0), ("gw", 0, 1), ("r", 0, 0, 0),
-    ("b", 0, 1, 0), ("s1", 0, 0, 1), ("gs", 1, 0), ("b2", 0, 1, 0), ("b", 0, 1, 1),
-    ("s1", 0, 0, 0), ("gw", 1, 1), ("b2", 0, 1, 1), ("s2", 0, 0, 1), ("r", 0, 1, 0),
-    ("b", 1, 1, 1), ("gw", 1, 0), ("b", 1, 1, 0), ("r", 0, 1, 1), ("b", 1, 0, 0),
-    ("s2", 0, 0, 0), ("g1", 0, 0, 1), ("s1", 0, 1, 0), ("b2", 1, 1, 1), ("r", 1, 1, 1),
-    ("r", 1, 1, 0), ("b2", 1, 1, 0), ("b", 1, 0, 1), ("g1", 0, 0, 0), ("s1", 0, 1, 1),
-    ("b2", 1, 0, 1), ("s2", 0, 1, 0), ("s1", 1, 1, 0), ("b2", 1, 0, 0), ("g2", 0, 0, 1),
-    ("r", 1, 0, 0), ("r", 1, 0, 1), ("s1", 1, 1, 1), ("s2", 0, 1, 1), ("g2", 0, 0, 0),
-    ("g1", 0, 1, 0), ("s2", 1, 1, 0), ("s2", 1, 1, 1), ("s1", 1, 0, 0), ("g1", 0, 1, 1),
-    ("s1", 1, 0, 1), ("f", 0, 0, 1), ("g2", 0, 1, 0), ("g1", 1, 1, 0), ("g2", 0, 1, 1),
-    ("g1", 1, 1, 1), ("f", 0, 0, 0), ("z", 0, 0, 1), ("s2", 1, 0, 1), ("s2", 1, 0, 0),
-    ("f", 0, 1, 1), ("g2", 1, 1, 0), ("z", 0, 0, 0), ("z", 0, 1, 1), ("g2", 1, 1, 1),
-    ("f", 0, 1, 0), ("z", 0, 1, 0), ("g1", 1, 0, 0), ("g1", 1, 0, 1), ("f", 1, 1, 0),
-    ("g2", 1, 0, 0), ("g2", 1, 0, 1), ("out", 0, 1, 1), ("z", 1, 1, 0), ("f", 1, 1, 1),
-    ("z", 1, 1, 1), ("f", 1, 0, 1), ("f", 1, 0, 0), ("out", 0, 1, 0), ("z", 1, 0, 1),
-    ("out", 0, 0, 1), ("z", 1, 0, 0), ("out", 1, 1, 0), ("out", 1, 1, 1), ("out", 0, 0, 0),
-    ("out", 1, 0, 1), ("out", 1, 0, 0),
+    ("gs", 0, 0), ("gs", 0, 1), ("gw", 0, 0), ("b", 0, 0, 0), ("b", 0, 0, 1), ("gs", 1, 1),
+    ("b2", 0, 0, 0), ("b2", 0, 0, 1), ("gw", 0, 1), ("r", 0, 0, 0), ("r", 0, 0, 1),
+    ("b", 0, 1, 0), ("b2", 0, 1, 0), ("b", 0, 1, 1), ("gs", 1, 0), ("s1", 0, 0, 0),
+    ("s1", 0, 0, 1), ("b2", 0, 1, 1), ("r", 0, 1, 0), ("gw", 1, 1), ("r", 0, 1, 1),
+    ("s2", 0, 0, 1), ("gw", 1, 0), ("b", 1, 1, 0), ("b", 1, 1, 1), ("b2", 1, 1, 1),
+    ("b", 1, 0, 1), ("b2", 1, 1, 0), ("s2", 0, 0, 0), ("b", 1, 0, 0), ("g0", 0, 0, 1),
+    ("s1", 0, 1, 0), ("r", 1, 1, 0), ("r", 1, 1, 1), ("s1", 0, 1, 1), ("r", 1, 0, 0),
+    ("b2", 1, 0, 0), ("g0", 0, 0, 0), ("b2", 1, 0, 1), ("s2", 0, 1, 0), ("s1", 1, 1, 0),
+    ("r", 1, 0, 1), ("s2", 0, 1, 1), ("g1", 0, 0, 0), ("s1", 1, 1, 1), ("g1", 0, 0, 1),
+    ("g0", 0, 1, 0), ("s1", 1, 0, 1), ("g0", 0, 1, 1), ("s1", 1, 0, 0), ("s2", 1, 1, 0),
+    ("s2", 1, 1, 1), ("g2", 0, 0, 1), ("g2", 0, 0, 0), ("g1", 0, 1, 0), ("g1", 0, 1, 1),
+    ("g0", 1, 1, 0), ("g0", 1, 1, 1), ("s2", 1, 0, 0), ("f", 0, 0, 1, 1), ("f", 0, 0, 1, 0),
+    ("p", 0, 0, 1), ("g2", 0, 1, 1), ("g2", 0, 1, 0), ("f", 0, 0, 0, 1), ("s2", 1, 0, 1),
+    ("f", 0, 0, 0, 0), ("z", 0, 0, 1), ("p", 0, 0, 0), ("g1", 1, 1, 0), ("g1", 1, 1, 1),
+    ("f", 0, 1, 1, 1), ("f", 0, 1, 1, 0), ("p", 0, 1, 1), ("f", 0, 1, 0, 1), ("z", 0, 0, 0),
+    ("g0", 1, 0, 1), ("f", 0, 1, 0, 0), ("g0", 1, 0, 0), ("z", 0, 1, 1), ("p", 0, 1, 0),
+    ("g2", 1, 1, 1), ("g2", 1, 1, 0), ("g1", 1, 0, 1), ("g1", 1, 0, 0), ("z", 0, 1, 0),
+    ("f", 1, 1, 1, 1), ("f", 1, 1, 1, 0), ("p", 1, 1, 1), ("f", 1, 1, 0, 0), ("f", 1, 1, 0, 1),
+    ("g2", 1, 0, 1), ("z", 1, 1, 1), ("out", 0, 1, 1), ("g2", 1, 0, 0), ("p", 1, 1, 0),
+    ("out", 0, 1, 0), ("z", 1, 1, 0), ("f", 1, 0, 0, 1), ("f", 1, 0, 1, 1), ("f", 1, 0, 1, 0),
+    ("out", 0, 0, 0), ("p", 1, 0, 1), ("out", 0, 0, 1), ("f", 1, 0, 0, 0), ("p", 1, 0, 0),
+    ("z", 1, 0, 1), ("z", 1, 0, 0), ("out", 1, 1, 1), ("out", 1, 1, 0), ("out", 1, 0, 1),
+    ("out", 1, 0, 0),
 )
 
 
@@ -189,14 +195,8 @@
             full[g, :, :, :, cols] = term
             send[g, :, :, :, cols] = term.astype(jnp.bfloat16)
 
-        count = extent // TILE
-
-        @pl.loop(0, count)
-        def _(n):
-            tile(pl.multiple_of(start + n * TILE, 128), TILE)
-
-        if extent % TILE:
-            tile(start + count * TILE, extent % TILE)
+        for first in range(start, start + extent, TILE):
+            tile(first, min(TILE, start + extent - first))
 
     kinds = (
         (span2, full_p, send1_p, recv1_p, relay_p, send2_p, recv2_p, own2_p),
@@ -309,19 +309,23 @@
     def ag_bufs(q):
         return (hidden, span1) if q == 0 else (grads, span2)
 
-    def ag1_copies(q, g, o):
+    def spot(g, o, step):
+        device, place = cross(g, o, step)
+        return device, (x, place) if along_x(g, o) else (place, y)
+
+    def ag1_start(q, g, o):
         buf, span = ag_bufs(q)
         mine = buf.at[g, x, y, :, span[o]]
-        return [
-            remote(
-                mine,
-                mine,
-                "ag1",
-                (q, g, o),
-                cross(g, o, d)[0],
-            )
-            for d in range(1, NX)
-        ]
+        for step in (1, -1):
+            go(remote(mine, mine, "ag1", (q, g, o), spot(g, o, step)[0]))
+
+    def step_g0(q, g, o):
+        buf, span = ag_bufs(q)
+        arrive(buf.at[g, 0, pl.ds(0, 2), :, span[o]], "ag1", (q, g, o))
+        head = (span[o].size // 128 + 1) // 2 * 128
+        for step, start, size in ((1, 0, head), (-1, head, span[o].size - head)):
+            block = buf.at[(g, *spot(g, o, -step)[1], slice(None), pl.ds(span[o].start + start, size))]
+            go(remote(block, block, "ag1on", (q, g, o), spot(g, o, step)[0]))
 
     def ag2_copies(q, g, o):
         buf, span = ag_bufs(q)
@@ -369,12 +373,11 @@
                 total * up * sigmoid * (1.0 + gate * (1.0 - sigmoid))
             ).astype(jnp.bfloat16)
             grads[g, x, y, :, second] = (total * gate * sigmoid).astype(jnp.bfloat16)
-        for copy in ag1_copies(q, g, o):
-            go(copy)
+        ag1_start(q, g, o)
 
     def step_g1(q, g, o):
         buf, span = ag_bufs(q)
-        arrive(buf.at[g, 0, pl.ds(0, NX - 1), :, span[o]], "ag1", (q, g, o))
+        arrive(buf.at[g, 0, 0, :, span[o]], "ag1on", (q, g, o))
         for copy in ag2_copies(q, g, o)[:4]:
             go(copy)
 
@@ -399,30 +402,29 @@
             at(dk=1),
         )
 
-    def rows_there(q, g):
+    def step_f(q, g, c, o):
         buf, span = ag_bufs(q)
-        for o in range(2):
-            arrive(buf.at[g, pl.ds(0, 2), :, :, span[o]], "rest", (q, g, o))
-
-    def step_f(q, g, c):
-        once(("rows", q, g), lambda: rows_there(q, g))
-        buf, _ = ag_bufs(q)
-        left = buf[g].reshape(NB * HALF, buf.shape[-1])
-
+        once(
+            ("rows", q, g, o),
+            lambda: arrive(buf.at[g, pl.ds(0, 2), :, :, span[o]], "rest", (q, g, o)),
+        )
+        left = buf[g, :, :, :, span[o]].reshape(NB * HALF, span[o].size)
         strip = strip_of(q, g, c)
-
-        @pl.loop(0, strip.size // TILE)
-        def _(n):
-            cols = pl.ds(pl.multiple_of(strip.start + n * TILE, TILE), TILE)
+        more = ("part", q, g, c) in arrived
+        arrived.add(("part", q, g, c))
+        for n in range(strip.size // TILE):
+            cols = pl.ds(strip.start + n * TILE, TILE)
             if q == 0:
-                term = jnp.dot(left, down_w[:, cols], preferred_element_type=jnp.float32)
+                term = jnp.dot(left, down_w[span[o], cols], preferred_element_type=jnp.float32)
             else:
                 term = lax.dot_general(
-                    left, gu_w[cols, :], (((1,), (1,)), ((), ())),
+                    left, gu_w[cols, span[o]], (((1,), (1,)), ((), ())),
                     preferred_element_type=jnp.float32,
                 )
-            acc[q, g, :, :, :, cols] = term.reshape(NZ, 2, HALF, TILE)
-
+            term = term.reshape(NZ, 2, HALF, TILE)
+            acc[q, g, :, :, :, cols] = acc[q, g, :, :, :, cols] + term if more else term
+
+    def step_p(q, g, c):
         go(pair_copy(q, g, c))
 
     def z_copy(t, g, c, e):
@@ -478,7 +480,9 @@
         "r": step_r,
         "s1": step_s1,
         "s2": step_s2,
+        "g0": step_g0,
         "g1": step_g1,
+        "p": step_p,
         "g2": step_g2,
         "f": step_f,
         "z": step_z,
@@ -497,7 +501,8 @@
         depart(relay, "relay", (q,))
         depart(recv1, "rs1", (q,))
         depart(recv2, "rs2", (q,))
-        depart(buf.at[:, 0, pl.ds(0, NX - 1)], "ag1", (q,))
+        depart(buf.at[:, 0, pl.ds(0, 2)], "ag1", (q,))
+        depart(buf.at[:, 0, 0], "ag1on", (q,))
         depart(buf.at[:, 0], "first", (q,))
         depart(buf.at[:, pl.ds(0, 2)], "rest", (q,))
         depart(pair.at[q], "pair", (q,))

time: 96.7 us -> 93 us (0.962)
  Pallas kernels: 96 us -> 92.2 us
    pallas_call x1, Pallas kernels: 94.4 us -> 90.7 us  [body(): pl.pallas_call(functools.partial(kernel, split), name='swiglu_both_ways',...]
where the time goes in v4:
time: 93 us; the launch traced here: 92.9 us
  Pallas kernels  92.2 us (99%)
    pallas_call x1, Pallas kernels, body(): pl.pallas_call(functools.partial(kernel, split), name='swiglu_both_ways',...  90.7 us

profile of v4, /device:TPU:1, one launch (start us, length us, event | category | flops | bytes accessed | tf_op | source)
XLA Modules:
  0.0 92.9 jit_solution(15499594483828162979)
XLA Ops:
  0.6 90.7 %swiglu_both_ways.1 = bf16[2,2,16,1024]{3,2,1,0:T(8,128)(2,1)} custom-call(bf16[2,16,1024]{2,1,0:T(8,128)(2,1)} %bitcast.4, bf16[2,16,1024]{2,1,0:T(8,128)(2,1)} %bitcast.5, bf16[1024,1664]{1,0:T(8,128)(2,1)} %gate_weight.1, bf16[1024,1664]{1,0:T(8,128)(2,1)} %up_weight.1, bf16[1664,1024]{1,0:T(8,128)(2,1)} %down_weight.1), custom_call_target="tpu_custom_call" | custom-call | tf_op jit(solution)/shard_map/swiglu_both_ways/pallas_call | solution.py:552
  91.3 1.6 %finish.1 = (bf16[32,1024]{1,0:T(8,128)(2,1)}, bf16[32,1024]{1,0:T(8,128)(2,1)}) custom-call(bf16[2,32,1024]{2,1,0:T(8,128)(2,1)} %bitcast.3), custom_call_target="tpu_custom_call" | custom-call | tf_op jit(solution)/shard_map/finish/pallas_call | solution.py:570

commit v5 on v4

--- a/solution.py
+++ b/solution.py
@@ -12,6 +12,7 @@
 NB = NX * NY
 HALF = 16
 TILE = 256
+PARTS = 4
 GROUPS = (
     ((0, 2, 0, 0), (2, 2, -1, 0), (4, 2, 1, 0), (6, 1, 2, 0), (7, 1, -2, 0)),
     ((0, 1, 2, 1), (1, 1, -2, 1), (2, 2, 3, 0), (4, 2, -3, 0), (6, 2, 4, 0)),
@@ -21,13 +22,13 @@
 ARRIVALS = {
     "seen": (2, 2),
     "share": (2, 2),
-    "relay": (2, 2, 2),
-    "rs1": (2, 2, 2),
-    "rs2": (2, 2, 2),
-    "ag1": (2, 2, 2),
-    "ag1on": (2, 2, 2),
-    "first": (2, 2, 2),
-    "rest": (2, 2, 2),
+    "relay": (2, 2, PARTS),
+    "rs1": (2, 2, PARTS),
+    "rs2": (2, 2, PARTS),
+    "ag1": (2, 2, PARTS),
+    "ag1on": (2, 2, PARTS),
+    "first": (2, 2, PARTS),
+    "rest": (2, 2, PARTS),
     "pair": (2, 2, 2),
     "z": (2, 2, 2),
 }
@@ -36,34 +37,50 @@
 LAST = (0, 0)
 STRIPS = ((2, 2), (2, 2))
 SCHEDULE = (
-    ("gs", 0, 0), ("gs", 0, 1), ("gw", 0, 0), ("b", 0, 0, 0), ("b", 0, 0, 1), ("gs", 1, 1),
-    ("b2", 0, 0, 0), ("b2", 0, 0, 1), ("gw", 0, 1), ("r", 0, 0, 0), ("r", 0, 0, 1),
-    ("b", 0, 1, 0), ("b2", 0, 1, 0), ("b", 0, 1, 1), ("gs", 1, 0), ("s1", 0, 0, 0),
-    ("s1", 0, 0, 1), ("b2", 0, 1, 1), ("r", 0, 1, 0), ("gw", 1, 1), ("r", 0, 1, 1),
-    ("s2", 0, 0, 1), ("gw", 1, 0), ("b", 1, 1, 0), ("b", 1, 1, 1), ("b2", 1, 1, 1),
-    ("b", 1, 0, 1), ("b2", 1, 1, 0), ("s2", 0, 0, 0), ("b", 1, 0, 0), ("g0", 0, 0, 1),
-    ("s1", 0, 1, 0), ("r", 1, 1, 0), ("r", 1, 1, 1), ("s1", 0, 1, 1), ("r", 1, 0, 0),
-    ("b2", 1, 0, 0), ("g0", 0, 0, 0), ("b2", 1, 0, 1), ("s2", 0, 1, 0), ("s1", 1, 1, 0),
-    ("r", 1, 0, 1), ("s2", 0, 1, 1), ("g1", 0, 0, 0), ("s1", 1, 1, 1), ("g1", 0, 0, 1),
-    ("g0", 0, 1, 0), ("s1", 1, 0, 1), ("g0", 0, 1, 1), ("s1", 1, 0, 0), ("s2", 1, 1, 0),
-    ("s2", 1, 1, 1), ("g2", 0, 0, 1), ("g2", 0, 0, 0), ("g1", 0, 1, 0), ("g1", 0, 1, 1),
-    ("g0", 1, 1, 0), ("g0", 1, 1, 1), ("s2", 1, 0, 0), ("f", 0, 0, 1, 1), ("f", 0, 0, 1, 0),
-    ("p", 0, 0, 1), ("g2", 0, 1, 1), ("g2", 0, 1, 0), ("f", 0, 0, 0, 1), ("s2", 1, 0, 1),
-    ("f", 0, 0, 0, 0), ("z", 0, 0, 1), ("p", 0, 0, 0), ("g1", 1, 1, 0), ("g1", 1, 1, 1),
-    ("f", 0, 1, 1, 1), ("f", 0, 1, 1, 0), ("p", 0, 1, 1), ("f", 0, 1, 0, 1), ("z", 0, 0, 0),
-    ("g0", 1, 0, 1), ("f", 0, 1, 0, 0), ("g0", 1, 0, 0), ("z", 0, 1, 1), ("p", 0, 1, 0),
-    ("g2", 1, 1, 1), ("g2", 1, 1, 0), ("g1", 1, 0, 1), ("g1", 1, 0, 0), ("z", 0, 1, 0),
-    ("f", 1, 1, 1, 1), ("f", 1, 1, 1, 0), ("p", 1, 1, 1), ("f", 1, 1, 0, 0), ("f", 1, 1, 0, 1),
-    ("g2", 1, 0, 1), ("z", 1, 1, 1), ("out", 0, 1, 1), ("g2", 1, 0, 0), ("p", 1, 1, 0),
-    ("out", 0, 1, 0), ("z", 1, 1, 0), ("f", 1, 0, 0, 1), ("f", 1, 0, 1, 1), ("f", 1, 0, 1, 0),
-    ("out", 0, 0, 0), ("p", 1, 0, 1), ("out", 0, 0, 1), ("f", 1, 0, 0, 0), ("p", 1, 0, 0),
-    ("z", 1, 0, 1), ("z", 1, 0, 0), ("out", 1, 1, 1), ("out", 1, 1, 0), ("out", 1, 0, 1),
-    ("out", 1, 0, 0),
+    ("gs", 0, 0), ("gs", 1, 0), ("gs", 0, 1), ("gs", 1, 1), ("gw", 0, 0), ("b", 0, 0, 2),
+    ("b", 0, 0, 1), ("b", 0, 0, 0), ("b", 0, 0, 3), ("b2", 0, 0, 2), ("b2", 0, 0, 0),
+    ("b2", 0, 0, 1), ("gw", 1, 0), ("b2", 0, 0, 3), ("r", 0, 0, 2), ("b", 1, 0, 1),
+    ("r", 0, 0, 1), ("r", 0, 0, 0), ("r", 0, 0, 3), ("b2", 1, 0, 1), ("b", 1, 0, 2),
+    ("b", 1, 0, 0), ("b2", 1, 0, 0), ("b", 1, 0, 3), ("b2", 1, 0, 3), ("r", 1, 0, 1),
+    ("s1", 0, 0, 2), ("gw", 0, 1), ("s1", 0, 0, 1), ("s1", 0, 0, 0), ("s1", 0, 0, 3),
+    ("b", 0, 1, 1), ("b", 0, 1, 2), ("b", 0, 1, 3), ("b", 0, 1, 0), ("s1", 1, 0, 1),
+    ("b2", 0, 1, 1), ("r", 1, 0, 0), ("b2", 0, 1, 0), ("b2", 0, 1, 2), ("r", 0, 1, 1),
+    ("s2", 0, 0, 3), ("r", 0, 1, 2), ("r", 0, 1, 3), ("s2", 0, 0, 1), ("gw", 1, 1),
+    ("b2", 0, 1, 3), ("r", 0, 1, 0), ("s2", 0, 0, 0), ("s2", 0, 0, 2), ("b", 1, 1, 1),
+    ("b", 1, 1, 2), ("b", 1, 1, 3), ("b2", 1, 1, 3), ("s1", 0, 1, 1), ("s1", 0, 1, 2),
+    ("b2", 1, 1, 2), ("b", 1, 1, 0), ("g0", 0, 0, 3), ("s1", 0, 1, 0), ("g0", 0, 0, 0),
+    ("s1", 0, 1, 3), ("r", 1, 1, 1), ("r", 1, 1, 2), ("g0", 0, 0, 2), ("b2", 1, 1, 0),
+    ("b2", 1, 1, 1), ("r", 1, 1, 3), ("s2", 0, 1, 1), ("g0", 0, 0, 1), ("s2", 0, 1, 2),
+    ("r", 1, 0, 3), ("r", 1, 1, 0), ("g1", 0, 0, 0), ("g1", 0, 0, 3), ("s2", 0, 1, 0),
+    ("s1", 1, 1, 2), ("g1", 0, 0, 2), ("s2", 0, 1, 3), ("s1", 1, 1, 1), ("s1", 1, 1, 3),
+    ("g0", 0, 1, 2), ("b2", 1, 0, 2), ("s1", 1, 0, 0), ("s1", 1, 1, 0), ("g0", 0, 1, 1),
+    ("g1", 0, 0, 1), ("r", 1, 0, 2), ("g0", 0, 1, 0), ("g2", 0, 0, 3), ("s2", 1, 1, 2),
+    ("g2", 0, 0, 0), ("g0", 0, 1, 3), ("s2", 1, 1, 1), ("s2", 1, 1, 3), ("g1", 0, 1, 2),
+    ("g2", 0, 0, 2), ("g1", 0, 1, 1), ("g2", 0, 0, 1), ("s2", 1, 1, 0), ("g1", 0, 1, 0),
+    ("g0", 1, 1, 2), ("f", 0, 0, 1, 3), ("g1", 0, 1, 3), ("f", 0, 0, 1, 0), ("g0", 1, 1, 3),
+    ("s1", 1, 0, 2), ("s2", 1, 0, 0), ("s1", 1, 0, 3), ("g2", 0, 1, 1), ("f", 0, 0, 0, 0),
+    ("g0", 1, 1, 1), ("g2", 0, 1, 2), ("f", 0, 0, 0, 3), ("s2", 1, 0, 1), ("f", 0, 0, 1, 2),
+    ("f", 0, 0, 0, 2), ("f", 0, 0, 0, 1), ("g0", 1, 1, 0), ("p", 0, 0, 0), ("f", 0, 0, 1, 1),
+    ("g2", 0, 1, 0), ("p", 0, 0, 1), ("g1", 1, 1, 2), ("g2", 0, 1, 3), ("g1", 1, 1, 3),
+    ("f", 0, 1, 1, 1), ("z", 0, 0, 0), ("s2", 1, 0, 2), ("s2", 1, 0, 3), ("z", 0, 0, 1),
+    ("g1", 1, 1, 0), ("g1", 1, 1, 1), ("f", 0, 1, 1, 2), ("f", 0, 1, 1, 0), ("g0", 1, 0, 1),
+    ("f", 0, 1, 1, 3), ("p", 0, 1, 1), ("g0", 1, 0, 0), ("g2", 1, 1, 3), ("f", 0, 1, 0, 3),
+    ("f", 0, 1, 0, 0), ("f", 0, 1, 0, 1), ("z", 0, 1, 1), ("g2", 1, 1, 2), ("g0", 1, 0, 3),
+    ("g0", 1, 0, 2), ("g2", 1, 1, 0), ("g2", 1, 1, 1), ("f", 0, 1, 0, 2), ("p", 0, 1, 0),
+    ("g1", 1, 0, 0), ("g1", 1, 0, 1), ("z", 0, 1, 0), ("f", 1, 1, 1, 2), ("g1", 1, 0, 3),
+    ("g1", 1, 0, 2), ("f", 1, 1, 1, 3), ("f", 1, 1, 0, 2), ("f", 1, 1, 1, 1),
+    ("f", 1, 1, 1, 0), ("p", 1, 1, 1), ("g2", 1, 0, 1), ("g2", 1, 0, 0), ("z", 1, 1, 1),
+    ("f", 1, 1, 0, 3), ("f", 1, 1, 0, 0), ("g2", 1, 0, 3), ("g2", 1, 0, 2), ("f", 1, 1, 0, 1),
+    ("p", 1, 1, 0), ("f", 1, 0, 1, 1), ("f", 1, 0, 0, 1), ("z", 1, 1, 0), ("out", 0, 1, 1),
+    ("f", 1, 0, 0, 0), ("out", 0, 1, 0), ("f", 1, 0, 1, 3), ("f", 1, 0, 0, 3),
+    ("f", 1, 0, 0, 2), ("p", 1, 0, 0), ("f", 1, 0, 1, 2), ("out", 0, 0, 0), ("f", 1, 0, 1, 0),
+    ("p", 1, 0, 1), ("z", 1, 0, 0), ("z", 1, 0, 1), ("out", 0, 0, 1), ("out", 1, 1, 1),
+    ("out", 1, 1, 0), ("out", 1, 0, 0), ("out", 1, 0, 1),
 )
 
 
 def kernel(
-    split,
+    widths,
     tokens,
     cotangent,
     gate_weight,
@@ -98,7 +115,6 @@
     load_sem,
     *sems,
 ):
-    width = gate_weight.shape[1]
     row, col = lax.axis_index("row"), lax.axis_index("col")
     x, y = row // NY, row % NY
     z, k = col // 2, col % 2
@@ -127,10 +143,9 @@
         index = (*index, 0, 0)[: len(ARRIVALS[kind])]
         remote(like, like, kind, index, at(dk=1)).wait_send()
 
-    offset = (0, split)
-    widths = (split, width - split)
-    span1 = tuple(pl.ds(offset[o], widths[o]) for o in range(2))
-    span2 = tuple(pl.ds(2 * offset[o], 2 * widths[o]) for o in range(2))
+    offset = tuple(sum(widths[:o]) for o in range(PARTS))
+    span1 = tuple(pl.ds(offset[o], widths[o]) for o in range(PARTS))
+    span2 = tuple(pl.ds(2 * offset[o], 2 * widths[o]) for o in range(PARTS))
 
     loads = [
         pltpu.make_async_copy(src, dst, load_sem.at[i])
@@ -141,7 +156,7 @@
                     src.at[:, span1[o]],
                     gu_w.at[:, pl.ds(2 * offset[o] + p * widths[o], widths[o])],
                 )
-                for o in range(2)
+                for o in range(PARTS)
                 for p, src in enumerate((gate_weight, up_weight))
             ]
             + [(down_weight, down_w)]
@@ -251,7 +266,7 @@
 
     def step_b(q, g, o):
         once(("seen", q, g), lambda: tokens_there(q, g))
-        for n in (6,) if q else (2, 3, 4, 5):
+        for n in (2 + 2 * PARTS,) if q else (2 + 2 * o, 3 + 2 * o):
             once(("load", n), loads[n].wait)
         left = seen[q, g].reshape(NB * HALF, seen.shape[-1])
         if q == 0:
@@ -516,7 +531,8 @@
 def body(tokens, cotangent, gate_weight, up_weight, down_weight):
     rows, depth = tokens.shape
     width = gate_weight.shape[1]
-    split = (width // 128 + 1) // 2 * 128
+    lanes, more = divmod(width // 128, PARTS)
+    widths = tuple(128 * (lanes + (o < more)) for o in range(PARTS))
     bf16, f32, dma = jnp.bfloat16, jnp.float32, pltpu.SemaphoreType.DMA
     vmem = pltpu.VMEM
     assert rows == 2 * HALF
@@ -546,11 +562,11 @@
         vmem((2, 2, NZ, HALF, depth), bf16),
         vmem((2, 2, NZ, HALF, depth), bf16),
         vmem((2, 2, HALF, depth), f32),
-        dma((7,)),
+        dma((3 + 2 * PARTS,)),
     ]
     scratch += [dma(shapes[kind]) for kind in KINDS for shapes in (DEPARTURES, ARRIVALS)]
     both_out = pl.pallas_call(
-        functools.partial(kernel, split),
+        functools.partial(kernel, widths),
         name="swiglu_both_ways",
         out_shape=jax.ShapeDtypeStruct((2, 2, HALF, depth), bf16),
         in_specs=[pl.BlockSpec(memory_space=pl.ANY)] * 5,

time: 93 us -> 92.4 us (level)
  no operation moved by 1% of the time
where the time goes in v5:
time: 92.4 us; the launch traced here: 92.3 us
  Pallas kernels  91.6 us (99%)
    pallas_call x1, Pallas kernels, body(): pl.pallas_call(functools.partial(kernel, widths), name='swiglu_both_ways'...  90.1 us

profile of v5, /device:TPU:1, one launch (start us, length us, event | category | flops | bytes accessed | tf_op | source)
XLA Modules:
  0.0 92.3 jit_solution(8447732310351664337)
XLA Ops:
  0.6 90.1 %swiglu_both_ways.1 = bf16[2,2,16,1024]{3,2,1,0:T(8,128)(2,1)} custom-call(bf16[2,16,1024]{2,1,0:T(8,128)(2,1)} %bitcast.4, bf16[2,16,1024]{2,1,0:T(8,128)(2,1)} %bitcast.5, bf16[1024,1664]{1,0:T(8,128)(2,1)} %gate_weight.1, bf16[1024,1664]{1,0:T(8,128)(2,1)} %up_weight.1, bf16[1664,1024]{1,0:T(8,128)(2,1)} %down_weight.1), custom_call_target="tpu_custom_call" | custom-call | tf_op jit(solution)/shard_map/swiglu_both_ways/pallas_call | solution.py:568
  90.7 1.6 %finish.1 = (bf16[32,1024]{1,0:T(8,128)(2,1)}, bf16[32,1024]{1,0:T(8,128)(2,1)}) custom-call(bf16[2,32,1024]{2,1,0:T(8,128)(2,1)} %bitcast.3), custom_call_target="tpu_custom_call" | custom-call | tf_op jit(solution)/shard_map/finish/pallas_call | solution.py:586
